TPU v7x, 32 devices: a whole 2x2x4 slice. The times are simulated.
32 devices in a mesh: cfg: 2 (over x), work: 16 (over z, y, core).
Axes of the slice: x: 2, y: 2, z: 4, core: 2. Of those that a mesh axis runs over, the one named last changes fastest.
Arguments:
- sources: bfloat16 [32, 16384, 128], P('cfg', 'work'), parts along dimension 0, may hold values from -6 to 6
- perambs: bfloat16 [192, 16384], P('cfg', 'work'), parts along dimension 0, may hold values from -0.5 to 0.5
- source_ids: int32 [16], replicated, may hold values from 0 to 15
- peramb_ids: int32 [48, 3], replicated, may hold values from 0 to 95
- sink_counts: int32 [16], replicated, may hold values from 1 to 6, 48 in all
- weights: float32 [48], replicated, may hold values from -2 to 2, as said below
Outputs:
- sink_tensors: bfloat16 [32, 16384, 128], P(('cfg', 'work')), parts along dimension 0
There are 2 independent parts, one for each index of `cfg`. A program takes and returns all parts, laid end to end along the dimension named above; an argument that names none is the same for every part. Nothing has to cross between parts.
Inputs may be any that keep to these rules, and one draw needn't show every extreme that they name: `sink_counts`: diagrams are listed sink by sink in order; the counts add up to 48 and some sink has exactly 6 diagrams. `weights`: nonzero multiples of 1/4.
All inputs are finite; a program needn't handle non-finite values.
Results may differ from a plain program's by a relative error of at most 0.0064.
Values may be sent and summed in bfloat16 or wider, within the bound.
No kernel may reach another device: no remote copies, remote signals or barrier semaphores. Data moves between devices by JAX's collectives and lax.ppermute only.
A program may use at most 128 MiB of HBM per device.

v0:
```python
import functools

import jax
import jax.numpy as jnp
from jax import lax
from jax.experimental import pallas as pl
from jax.experimental.pallas import tpu as pltpu
from jax.sharding import PartitionSpec as P

MOST = 6
LEGS = 3
UNIT_ROWS = 16
B_BLOCK = 64
ACC = jnp.bfloat16
GROUPS = ((0, 1, 2, 3), (4, 5), (6,), (7,))
IN_FLIGHT = 5
FAR_TURNS = (2, 4)
VMEM = 36 * 1024 * 1024
SMALL_VMEM = 16 * 1024 * 1024


def pieces_kernel(shifts, ids_ref, source_ref, *refs):
    piece_refs, (held_ref, in_sems, out_sems) = refs[: len(shifts)], refs[len(shifts) :]
    own = lax.axis_index("work")
    reads, writes = [], []
    for i, shift in enumerate(shifts):
        reads.append(
            pltpu.make_async_copy(
                source_ref.at[ids_ref[own ^ shift]], held_ref.at[i], in_sems.at[i]
            )
        )
        writes.append(pltpu.make_async_copy(held_ref.at[i], piece_refs[i], out_sems.at[i]))
        reads[i].start()
    for read, write in zip(reads, writes):
        read.wait()
        write.start()
    for write in writes:
        write.wait()


def choose_pieces(sources, source_ids, shifts):
    return pl.pallas_call(
        functools.partial(pieces_kernel, shifts),
        in_specs=[pl.BlockSpec(memory_space=pltpu.SMEM), pl.BlockSpec(memory_space=pl.ANY)],
        out_specs=[pl.BlockSpec(memory_space=pl.ANY)] * len(shifts),
        out_shape=[jax.ShapeDtypeStruct(sources.shape[1:], sources.dtype)] * len(shifts),
        scratch_shapes=[
            pltpu.VMEM((len(shifts), *sources.shape[1:]), sources.dtype),
            pltpu.SemaphoreType.DMA((len(shifts),)),
            pltpu.SemaphoreType.DMA((len(shifts),)),
        ],
        compiler_params=pltpu.CompilerParams(vmem_limit_bytes=SMALL_VMEM),
    )(source_ids, sources)


def matrices_kernel(workers, counts_ref, matrix_ids_ref, peramb_ref, matrix_ref, choice_ref, spread_ref):
    rows = MOST * LEGS
    diagrams = matrix_ids_ref.shape[1]
    total = peramb_ref.shape[0]
    lanes = lax.broadcasted_iota(jnp.int32, (1, total), 1)

    def mark(sink, start):
        for slot in range(MOST):
            diagram = jnp.minimum(start + slot, diagrams - 1)
            for leg in range(LEGS):
                choice_ref[pl.ds(sink * rows + slot * LEGS + leg, 1), :] = jnp.where(
                    lanes == matrix_ids_ref[leg, diagram], 1.0, 0.0
                )
        return start + counts_ref[sink]

    lax.fori_loop(0, workers, mark, 0)
    chosen = jnp.dot(
        choice_ref[...].astype(jnp.bfloat16), peramb_ref[...], preferred_element_type=jnp.float32
    )
    extent = matrix_ref.shape[2]
    a_per = peramb_ref.shape[1] // extent
    for row in range(a_per):
        spread_ref[pl.ds(row, workers * rows, stride=a_per), :] = chosen[
            :, row * extent : (row + 1) * extent
        ]
    matrix_ref[...] = spread_ref[...].reshape(matrix_ref.shape).astype(jnp.bfloat16)


def choose_matrices(perambs, peramb_ids, sink_counts, workers, extent):
    rows = MOST * LEGS
    a_per = perambs.shape[1] // extent
    smem = pl.BlockSpec(memory_space=pltpu.SMEM)
    vmem = pl.BlockSpec(memory_space=pltpu.VMEM)
    return pl.pallas_call(
        functools.partial(matrices_kernel, workers),
        in_specs=[smem, smem, vmem],
        out_specs=vmem,
        out_shape=jax.ShapeDtypeStruct((workers, rows * a_per, extent), jnp.bfloat16),
        scratch_shapes=[
            pltpu.VMEM((workers * rows, perambs.shape[0]), jnp.float32),
            pltpu.VMEM((workers * rows * a_per, extent), jnp.float32),
        ],
        compiler_params=pltpu.CompilerParams(vmem_limit_bytes=SMALL_VMEM),
    )(sink_counts, peramb_ids.T, perambs)


def legs_kernel(
    workers, counts_ref, weights_ref, matrix_ref, leg3_ref, leg2_ref, leg1_ref, flat_ref, leg_ref
):
    extent = matrix_ref.shape[2]
    rows = MOST * LEGS
    a_per = matrix_ref.shape[1] // rows
    flat_ref[...] = matrix_ref[...].astype(jnp.float32).reshape(flat_ref.shape)
    own = lax.axis_index("work")
    start = lax.fori_loop(0, own, lambda i, total: total + counts_ref[i], 0)
    count = counts_ref[own]
    unit = UNIT_ROWS // a_per
    units = workers // unit
    for slot in range(MOST):
        for leg in range(LEGS):
            base = (slot * LEGS + leg) * a_per
            for row in range(a_per):
                leg_ref[pl.ds(row, workers, stride=a_per), :] = flat_ref[
                    pl.ds(base + row, workers, stride=rows * a_per), :
                ]
            if leg == 2:
                leg3_ref[:, slot * extent : (slot + 1) * extent] = leg_ref[...].T.astype(
                    jnp.bfloat16
                )
            elif leg == 1:
                leg2_ref[slot * extent : (slot + 1) * extent, :] = leg_ref[...].astype(
                    jnp.bfloat16
                )
            else:
                diagram = jnp.minimum(start + slot, weights_ref.shape[0] - 1)
                factor = jnp.where(slot < count, weights_ref[diagram], 0.0)
                leg_ref[...] = (factor * leg_ref[...]).T
                for block in range(units):
                    place = (own // unit) ^ block
                    leg1_ref[block, slot * UNIT_ROWS : (slot + 1) * UNIT_ROWS, :] = leg_ref[
                        pl.ds(pl.multiple_of(place * UNIT_ROWS, UNIT_ROWS), UNIT_ROWS), :
                    ].astype(jnp.bfloat16)


def make_legs(matrices, sink_counts, weights, workers):
    extent = matrices.shape[2]
    a_per = extent // workers
    smem = pl.BlockSpec(memory_space=pltpu.SMEM)
    vmem = pl.BlockSpec(memory_space=pltpu.VMEM)
    return pl.pallas_call(
        functools.partial(legs_kernel, workers),
        in_specs=[smem, smem, vmem],
        out_specs=[vmem] * 3,
        out_shape=[
            jax.ShapeDtypeStruct((extent, MOST * extent), jnp.bfloat16),
            jax.ShapeDtypeStruct((MOST * extent, extent), jnp.bfloat16),
            jax.ShapeDtypeStruct(
                (extent // UNIT_ROWS, MOST * UNIT_ROWS, extent), jnp.bfloat16
            ),
        ],
        scratch_shapes=[
            pltpu.VMEM((matrices.shape[0] * matrices.shape[1], extent), jnp.float32),
            pltpu.VMEM((extent, extent), jnp.float32),
        ],
        compiler_params=pltpu.CompilerParams(vmem_limit_bytes=SMALL_VMEM),
    )(sink_counts, weights, matrices)


def group_kernel(first, last, units, per_unit, extent, *refs):
    pieces = len(units) * per_unit
    piece_refs = refs[:pieces]
    leg3_ref, leg2_ref, leg1_ref = refs[pieces : pieces + 3]
    refs = refs[pieces + 3 :]
    if not first:
        acc_ref, refs = refs[0], refs[1:]
    out_ref, turned_ref, outer_ref, across_ref, held_ref, sems = refs[:6]
    a_per = piece_refs[0].shape[0] // extent
    unit_depth = MOST * UNIT_ROWS
    depth = unit_depth * len(units)
    pitch = depth + 8
    step = pl.program_id(0)

    def fetch(piece):
        return pltpu.make_async_copy(piece_refs[piece], held_ref.at[piece], sems.at[piece])

    @pl.when(step == 0)
    def fetch_all():
        for piece in range(pieces):
            fetch(piece).start()

    def inner_legs(piece):
        place, lane = piece // per_unit, piece % per_unit
        fetch(piece).wait()
        sender = (lax.axis_index("work") & (per_unit - 1)) ^ lane
        third = jnp.dot(
            held_ref[piece], leg3_ref[...], preferred_element_type=jnp.float32
        ).astype(jnp.bfloat16)
        for d in range(MOST):
            columns = third[:, d * extent : (d + 1) * extent]
            wide = jnp.concatenate(
                [columns[a * extent : (a + 1) * extent] for a in range(a_per)], axis=1
            )
            second = jnp.dot(
                leg2_ref[d * extent : (d + 1) * extent, :],
                wide,
                preferred_element_type=jnp.float32,
            )
            for a in range(a_per):
                row = place * unit_depth + d * UNIT_ROWS + sender * a_per + a
                turned_ref[pl.ds(row, extent, stride=pitch), :] = second[
                    :, a * extent : (a + 1) * extent
                ]

    @pl.when(step == 0)
    def turn_outer():
        for place, unit in enumerate(units):
            outer_ref[place * unit_depth : (place + 1) * unit_depth, :] = leg1_ref[
                unit
            ].astype(jnp.float32)
        across_ref[...] = outer_ref[...].T.astype(jnp.bfloat16)

    for piece in range(pieces):
        pl.when(step == piece)(functools.partial(inner_legs, piece))

    @pl.when(step >= pieces)
    def outer_leg():
        begin = (step - pieces) * B_BLOCK
        wide = jnp.concatenate(
            [
                turned_ref[pl.ds(pl.multiple_of((begin + b) * pitch, 8), depth), :].astype(
                    jnp.bfloat16
                )
                for b in range(B_BLOCK)
            ],
            axis=1,
        )
        whole = jnp.dot(across_ref[...], wide, preferred_element_type=jnp.float32)
        for b in range(B_BLOCK):
            part = whole[:, b * extent : (b + 1) * extent]
            if not first:
                part = part + acc_ref[b].astype(jnp.float32)
            if last:
                refs[6][pl.ds(b, extent, stride=B_BLOCK + 8), :] = part
            else:
                out_ref[b] = part.astype(out_ref.dtype)
        if last:
            for a in range(extent):
                out_ref[a] = refs[6][pl.ds(a * (B_BLOCK + 8), B_BLOCK), :].astype(jnp.bfloat16)


def add_group(units, pieces, leg3, leg2, leg1, acc, last):
    extent = leg3.shape[0]
    count = len(pieces)
    per_unit = count // len(units)
    depth = MOST * UNIT_ROWS * len(units)
    first = acc is None
    blocks = extent // B_BLOCK

    def whole_spec(x):
        return pl.BlockSpec(x.shape, lambda i: (0,) * x.ndim)

    def block_of(i):
        return jnp.maximum(i - count, 0)

    operands = [*pieces, leg3, leg2, leg1]
    in_specs = [pl.BlockSpec(memory_space=pl.ANY)] * count
    in_specs += [whole_spec(x) for x in operands[count:]]
    if not first:
        operands.append(acc)
        in_specs.append(pl.BlockSpec((B_BLOCK, extent, extent), lambda i: (block_of(i), 0, 0)))
    scratch = [
        pltpu.VMEM((extent * (depth + 8), extent), jnp.float32),
        pltpu.VMEM((depth, extent), jnp.float32),
        pltpu.VMEM((extent, depth), jnp.bfloat16),
        pltpu.VMEM((count, *pieces[0].shape), jnp.bfloat16),
        pltpu.SemaphoreType.DMA((count,)),
    ]
    if last:
        out_shape = jax.ShapeDtypeStruct((extent, extent, extent), jnp.bfloat16)
        out_spec = pl.BlockSpec((extent, B_BLOCK, extent), lambda i: (0, block_of(i), 0))
        scratch.append(pltpu.VMEM((extent * (B_BLOCK + 8), extent), jnp.float32))
    else:
        out_shape = jax.ShapeDtypeStruct((extent, extent, extent), ACC)
        out_spec = pl.BlockSpec((B_BLOCK, extent, extent), lambda i: (block_of(i), 0, 0))
    rows = count * pieces[0].shape[0]
    return pl.pallas_call(
        functools.partial(group_kernel, first, last, units, per_unit, extent),
        grid=(count + blocks,),
        in_specs=in_specs,
        out_specs=out_spec,
        out_shape=out_shape,
        scratch_shapes=scratch,
        compiler_params=pltpu.CompilerParams(
            dimension_semantics=("arbitrary",), vmem_limit_bytes=VMEM
        ),
        cost_estimate=pl.CostEstimate(
            flops=6 * MOST * rows * extent * extent,
            bytes_accessed=12 * extent**3,
            transcendentals=0,
        ),
    )(*operands)


def per_device(sources, perambs, source_ids, peramb_ids, sink_counts, weights):
    workers = lax.axis_size("work")
    extent = sources.shape[2]
    per_unit = UNIT_ROWS * workers // extent
    half = workers // 2
    far = list(range(half, workers))
    near = [s for pair in zip(range(half // 2), range(half // 2, half)) for s in pair][1:]
    near = [1, *(s for s in near if s != 1)]
    order = []
    while far or near:
        take_far = far and (not near or len(order) % IN_FLIGHT in FAR_TURNS)
        order.append(far.pop(0) if take_far else near.pop(0))
    early, late = tuple(order[:IN_FLIGHT]), (0, *order[IN_FLIGHT:])
    pieces = dict(zip(early, choose_pieces(sources, source_ids, early)))
    pieces.update(zip(late, choose_pieces(sources, source_ids, late)))
    arrived = {0: pieces[0]}

    def send(place):
        shift = order[place]
        piece = pieces[shift]
        if place >= IN_FLIGHT:
            before = order[place - IN_FLIGHT]
            piece, arrived[before] = lax.optimization_barrier((piece, arrived[before]))
        arrived[shift] = lax.ppermute(piece, "work", [(i, i ^ shift) for i in range(workers)])

    for place in range(IN_FLIGHT):
        send(place)
    matrices = choose_matrices(perambs, peramb_ids, sink_counts, workers, extent)
    matrices = lax.all_to_all(matrices, "work", split_axis=0, concat_axis=0, tiled=True)
    leg3, leg2, leg1 = make_legs(matrices, sink_counts, weights, workers)
    for place in range(IN_FLIGHT, len(order)):
        send(place)

    acc = None
    for group, units in enumerate(GROUPS):
        members = [arrived[u * per_unit + lane] for u in units for lane in range(per_unit)]
        acc = add_group(units, members, leg3, leg2, leg1, acc, group == len(GROUPS) - 1)
    return acc.reshape(1, extent * extent, extent)


def solution(mesh):
    return jax.shard_map(
        per_device,
        mesh=mesh,
        in_specs=(P("cfg", "work", None), P("cfg", "work"), P(), P(), P(), P()),
        out_specs=P(("cfg", "work"), None, None),
        check_vma=False,
    )
```

profile of v0, /device:TPU:0, one launch (start us, length us, event | category | flops | bytes accessed | tf_op | source)
XLA Modules:
  0.0 127.3 jit_solution(4247486839985415997)
XLA Ops:
  0.0 0.9 copy-done.1
  2.3 2.2 %shard_map.66 = bf16[16,144,128]{2,1,0:T(8,128)(2,1)} custom-call(s32[16]{0:T(128)S(1)} %copy-done.4, s32[3,48]{1,0:T(4,128)S(1)} %bitcast.2, bf16[96,1024]{1,0:T(8,128)(2,1)S(1)} %copy-done.1), custom_call_target="tpu_custom_call" | custom-call | tf_op jit(solution)/shard_map/pallas_call | solution.py:89
  4.5 7.4 %all-to-all-start = ((bf16[16,144,128]{2,1,0:T(8,128)(2,1)}), bf16[16,144,128]{2,1,0:T(8,128)(2,1)S(1)}, u32[]{:S(2)}, u32[]{:S(2)}) async-start(bf16[16,144,128]{2,1,0:T(8,128)(2,1)} %shard_map.66), calls=%async_computation | async-start | bytes 1179648 | tf_op jit(solution)/shard_map/all_to_all | solution.py:327
  11.9 2.2 %copy-done = bf16[16,1024,128]{2,1,0:T(8,128)(2,1)S(1)} copy-done((bf16[16,1024,128]{2,1,0:T(8,128)(2,1)S(1)}, bf16[16,1024,128]{2,1,0:T(8,128)(2,1)}, u32[]{:S(2)}) %copy-start) | copy-done | bytes 4194328
  14.7 0.9 shard_map.65
  16.0 2.6 %collective-permute-start.9 = (bf16[1024,128]{1,0:T(8,128)(2,1)S(1)}, bf16[1024,128]{1,0:T(8,128)(2,1)S(1)}, u32[]{:S(2)}, u32[]{:S(2)}) collective-permute-start(bf16[1024,128]{1,0:T(8,128)(2,1)S(1)} %get-tuple-element.64), channel_id=1, source_target_pairs={{0,8},{1,9},{2,10},{3,11},{4,12},{5,13},{6,14},{7,15},{8,0},{9,1},... | collective-permute-start | bytes 786440 | tf_op jit(solution)/shard_map/ppermute | solution.py:322
  18.6 1.5 %collective-permute-start.6 = (bf16[1024,128]{1,0:T(8,128)(2,1)S(1)}, bf16[1024,128]{1,0:T(8,128)(2,1)S(1)}, u32[]{:S(2)}, u32[]{:S(2)}) collective-permute-start(bf16[1024,128]{1,0:T(8,128)(2,1)S(1)} %get-tuple-element.59), channel_id=1, source_target_pairs={{0,4},{1,5},{2,6},{3,7},{4,0},{5,1},{6,2},{7,3},{8,12},{9,13},{10,... | collective-permute-start | bytes 786440 | tf_op jit(solution)/shard_map/ppermute | solution.py:322
  20.7 2.0 %shard_map.64 = (bf16[1024,128]{1,0:T(8,128)(2,1)S(1)}, bf16[1024,128]{1,0:T(8,128)(2,1)S(1)}, bf16[1024,128]{1,0:T(8,128)(2,1)S(1)}, bf16[1024,128]{1,0:T(8,128...) custom-call(s32[16]{0:T(128)S(1)} %copy-done.3, ...), custom_call_target="tpu_custom_call" | custom-call | tf_op jit(solution)/shard_map/pallas_call | solution.py:42
  23.4 1.7 %collective-permute-start.13 = (bf16[1024,128]{1,0:T(8,128)(2,1)S(1)}, bf16[1024,128]{1,0:T(8,128)(2,1)S(1)}, u32[]{:S(2)}, u32[]{:S(2)}) collective-permute-start(bf16[1024,128]{1,0:T(8,128)(2,1)S(1)} %get-tuple-element.76), channel_id=1, source_target_pairs={{0,2},{1,3},{2,0},{3,1},{4,6},{5,7},{6,4},{7,5},{8,10},{9,11},{10,... | collective-permute-start | bytes 786440 | tf_op jit(solution)/shard_map/ppermute | solution.py:322
  25.1 20.8 %collective-permute-done.9.refs_0_ = bf16[1024,128]{1,0:T(8,128)(2,1)S(1)} collective-permute-done((bf16[1024,128]{1,0:T(8,128)(2,1)S(1)}, bf16[1024,128]{1,0:T(8,128)(2,1)S(1)}, u32[]{:S(2)}, u32[]{:S(2)}) %collective-permute-start.9) | collective-permute-done | bytes 262176 | tf_op jit(solution)/shard_map/ppermute | solution.py:322
  46.4 0.7 copy-done.7
  47.1 2.5 %collective-permute-start.7 = (bf16[1024,128]{1,0:T(8,128)(2,1)S(1)}, bf16[1024,128]{1,0:T(8,128)(2,1)S(1)}, u32[]{:S(2)}, u32[]{:S(2)}) collective-permute-start(bf16[1024,128]{1,0:T(8,128)(2,1)S(1)} %get-tuple-element.60), channel_id=1, source_target_pairs={{0,6},{1,7},{2,4},{3,5},{4,2},{5,3},{6,0},{7,1},{8,14},{9,15},{10,... | collective-permute-start | bytes 786440 | tf_op jit(solution)/shard_map/ppermute | solution.py:322
  49.6 6.7 %collective-permute-done.3.refs_1_ = bf16[1024,128]{1,0:T(8,128)(2,1)S(1)} collective-permute-done((bf16[1024,128]{1,0:T(8,128)(2,1)S(1)}, bf16[1024,128]{1,0:T(8,128)(2,1)S(1)}, u32[]{:S(2)}, u32[]{:S(2)}) %collective-permute-start.3) | collective-permute-done | bytes 262176 | tf_op jit(solution)/shard_map/ppermute | solution.py:322
  57.0 2.0 %collective-permute-start.1 = (bf16[1024,128]{1,0:T(8,128)(2,1)S(1)}, bf16[1024,128]{1,0:T(8,128)(2,1)S(1)}, u32[]{:S(2)}, u32[]{:S(2)}) collective-permute-start(bf16[1024,128]{1,0:T(8,128)(2,1)S(1)} %get-tuple-element.47), channel_id=1, source_target_pairs={{0,3},{1,2},{2,1},{3,0},{4,7},{5,6},{6,5},{7,4},{8,11},{9,10},{10,... | collective-permute-start | bytes 786440 | tf_op jit(solution)/shard_map/ppermute | solution.py:322
  59.8 2.5 %collective-permute-start.14 = (bf16[1024,128]{1,0:T(8,128)(2,1)}, bf16[1024,128]{1,0:T(8,128)(2,1)}, u32[]{:S(2)}, u32[]{:S(2)}) collective-permute-start(bf16[1024,128]{1,0:T(8,128)(2,1)} %get-tuple-element.82), channel_id=1, source_target_pairs={{0,7},{1,6},{2,5},{3,4},{4,3},{5,2},{6,1},{7,0},{8,15},{9,14},{10,... | collective-permute-start | bytes 786440 | tf_op jit(solution)/shard_map/ppermute | solution.py:322
  62.3 7.1 %collective-permute-done.10.refs_2_ = bf16[1024,128]{1,0:T(8,128)(2,1)S(1)} collective-permute-done((bf16[1024,128]{1,0:T(8,128)(2,1)S(1)}, bf16[1024,128]{1,0:T(8,128)(2,1)S(1)}, u32[]{:S(2)}, u32[]{:S(2)}) %collective-permute-start.10) | collective-permute-done | bytes 262176 | tf_op jit(solution)/shard_map/ppermute | solution.py:322
  69.6 0.7 copy-done.15
  70.3 2.4 %collective-permute-start.8 = (bf16[1024,128]{1,0:T(8,128)(2,1)}, bf16[1024,128]{1,0:T(8,128)(2,1)S(1)}, u32[]{:S(2)}, u32[]{:S(2)}) collective-permute-start(bf16[1024,128]{1,0:T(8,128)(2,1)} %get-tuple-element.61), channel_id=1, source_target_pairs={{0,12},{1,13},{2,14},{3,15},{4,8},{5,9},{6,10},{7,11},{8,4},{9,5},... | collective-permute-start | bytes 786440 | tf_op jit(solution)/shard_map/ppermute | solution.py:322
  72.6 12.7 %collective-permute-done.4.refs_3_ = bf16[1024,128]{1,0:T(8,128)(2,1)S(1)} collective-permute-done((bf16[1024,128]{1,0:T(8,128)(2,1)S(1)}, bf16[1024,128]{1,0:T(8,128)(2,1)S(1)}, u32[]{:S(2)}, u32[]{:S(2)}) %collective-permute-start.4) | collective-permute-done | bytes 262176 | tf_op jit(solution)/shard_map/ppermute | solution.py:322
  85.3 1.9 %collective-permute-start.5 = (bf16[1024,128]{1,0:T(8,128)(2,1)S(1)}, bf16[1024,128]{1,0:T(8,128)(2,1)S(1)}, u32[]{:S(2)}, u32[]{:S(2)}) collective-permute-start(bf16[1024,128]{1,0:T(8,128)(2,1)S(1)} %get-tuple-element.53), channel_id=1, source_target_pairs={{0,15},{1,14},{2,13},{3,12},{4,11},{5,10},{6,9},{7,8},{8,7},{9,6},... | collective-permute-start | bytes 786440 | tf_op jit(solution)/shard_map/ppermute | solution.py:322
  87.9 3.2 %collective-permute-start.2 = (bf16[1024,128]{1,0:T(8,128)(2,1)S(1)}, bf16[1024,128]{1,0:T(8,128)(2,1)S(1)}, u32[]{:S(2)}, u32[]{:S(2)}) collective-permute-start(bf16[1024,128]{1,0:T(8,128)(2,1)S(1)} %get-tuple-element.48), channel_id=1, source_target_pairs={{0,14},{1,15},{2,12},{3,13},{4,10},{5,11},{6,8},{7,9},{8,6},{9,7},... | collective-permute-start | bytes 786440 | tf_op jit(solution)/shard_map/ppermute | solution.py:322
  91.1 1.8 %shard_map.67 = (bf16[128,768]{1,0:T(8,128)(2,1)S(1)}, bf16[768,128]{1,0:T(8,128)(2,1)S(1)}, bf16[8,96,128]{2,1,0:T(8,128)(2,1)S(1)}) custom-call(s32[16]{0:T(128)S(1)} %copy-done.5, f32[48]{0:T(128)S(1)} %copy-done.6, bf16[16,144,128]{2,1,0:T(8,128)(2,1)S(1)} %all-to-all-done.matrix_ref), custom_call_target="tpu_custom_call" | custom-call | tf_op jit(solution)/shard_map/pallas_call | solution.py:145
  92.9 0.9 copy-done.8
  93.9 0.9 copy-done.10
  94.8 0.9 copy-done.12
  95.8 0.9 copy-done.14
  96.7 0.9 copy-done.16
  97.7 0.9 copy-done.18
  98.6 12.0 %shard_map.68.refs_7_ = bf16[128,128,128]{2,1,0:T(8,128)(2,1)S(1)} custom-call(bf16[1024,128]{1,0:T(8,128)(2,1)S(1)} %copy-done.12, bf16[1024,128]{1,0:T(8,128)(2,1)S(1)} %collective-permute-done.12.refs_1_, bf16[1024,128]{1,0:T(8,128)(2,1)S(1)} %copy-done.14, bf16[1024,128]{1,0:T(8,128)(2,1)S(1)} %copy-done.18, bf16[1024,128]{1,0:T(8,128)(2,1)S(1)} %copy-done.8, ...), custom_call_target="tpu_custom_call" | custom-call | flops 4831838208 | bytes 25165824 | tf_op jit(solution)/shard_map/pallas_call | solution.py:281
  110.6 6.4 %shard_map.69.refs_5_ = bf16[128,128,128]{2,1,0:T(8,128)(2,1)S(1)} custom-call(bf16[1024,128]{1,0:T(8,128)(2,1)S(1)} %collective-permute-done.9.refs_0_, bf16[1024,128]{1,0:T(8,128)(2,1)S(1)} %collective-permute-done.3.refs_1_, bf16[1024,128]{1,0:T(8,128)(2,1)S(1)} %collective-permute-done.10.refs_2_, bf16[1024,128]{1,0:T(8,128)(2,1)S(1)} %collective-permute-done.4.refs_3_, ...), custom_call_target="tpu_custom_call" | custom-call | flops 2415919104 | bytes 25165824 | tf_op jit(solution)/shard_map/pallas_call | solution.py:281
  117.0 3.8 %shard_map.70.refs_5_ = bf16[128,128,128]{2,1,0:T(8,128)(2,1)S(1)} custom-call(bf16[1024,128]{1,0:T(8,128)(2,1)S(1)} %collective-permute-done.8.refs_0_, bf16[1024,128]{1,0:T(8,128)(2,1)S(1)} %collective-permute-done.11.refs_1_, bf16[128,768]{1,0:T(8,128)(2,1)S(1)} %get-tuple-element.54.refs_8_.refs_4_.refs_2_, ...), custom_call_target="tpu_custom_call" | custom-call | flops 1207959552 | bytes 25165824 | tf_op jit(solution)/shard_map/pallas_call | solution.py:281
  120.9 6.3 %shard_map.71 = bf16[128,128,128]{2,1,0:T(8,128)(2,1)} custom-call(bf16[1024,128]{1,0:T(8,128)(2,1)S(1)} %collective-permute-done.2.refs_0_, bf16[1024,128]{1,0:T(8,128)(2,1)S(1)} %collective-permute-done.5.refs_1_, bf16[128,768]{1,0:T(8,128)(2,1)S(1)} %get-tuple-element.54.refs_8_.refs_4_.refs_2_, ...), custom_call_target="tpu_custom_call" | custom-call | flops 1207959552 | bytes 25165824 | tf_op jit(solution)/shard_map/pallas_call | solution.py:281
  (46 shorter events, 6.5 us)
Async XLA Ops:
  0.0 0.9 copy-start.1
  4.5 86.6 %all-to-all-start = ((bf16[16,144,128]{2,1,0:T(8,128)(2,1)}), bf16[16,144,128]{2,1,0:T(8,128)(2,1)S(1)}, u32[]{:S(2)}, u32[]{:S(2)}) async-start(bf16[16,144,128]{2,1,0:T(8,128)(2,1)} %shard_map.66), calls=%async_computation | async-start | bytes 1179648 | tf_op jit(solution)/shard_map/all_to_all | solution.py:327
  11.9 2.2 %copy-start = (bf16[16,1024,128]{2,1,0:T(8,128)(2,1)S(1)}, bf16[16,1024,128]{2,1,0:T(8,128)(2,1)}, u32[]{:S(2)}) copy-start(bf16[16,1024,128]{2,1,0:T(8,128)(2,1)} %source_ref.3) | copy-start | bytes 12582916
  14.7 76.4 %copy-start.5 = (s32[16]{0:T(128)S(1)}, s32[16]{0:T(128)}, u32[]{:S(2)}) copy-start(s32[16]{0:T(128)} %counts_ref.3) | copy-start | bytes 196
  14.7 76.4 %copy-start.6 = (f32[48]{0:T(128)S(1)}, f32[48]{0:T(128)}, u32[]{:S(2)}) copy-start(f32[48]{0:T(128)} %weights_ref.1) | copy-start | bytes 580
  15.6 7.9 %collective-permute-start.12 = (bf16[1024,128]{1,0:T(8,128)(2,1)S(1)}, bf16[1024,128]{1,0:T(8,128)(2,1)S(1)}, u32[]{:S(2)}, u32[]{:S(2)}) collective-permute-start(bf16[1024,128]{1,0:T(8,128)(2,1)S(1)} %get-tuple-element.73), channel_id=1, source_target_pairs={{0,1},{1,0},{2,3},{3,2},{4,5},{5,4},{6,7},{7,6},{8,9},{9,8},{10,11... | collective-permute-start | bytes 786440 | tf_op jit(solution)/shard_map/ppermute | solution.py:322
  16.0 29.9 %collective-permute-start.9 = (bf16[1024,128]{1,0:T(8,128)(2,1)S(1)}, bf16[1024,128]{1,0:T(8,128)(2,1)S(1)}, u32[]{:S(2)}, u32[]{:S(2)}) collective-permute-start(bf16[1024,128]{1,0:T(8,128)(2,1)S(1)} %get-tuple-element.64), channel_id=1, source_target_pairs={{0,8},{1,9},{2,10},{3,11},{4,12},{5,13},{6,14},{7,15},{8,0},{9,1},... | collective-permute-start | bytes 786440 | tf_op jit(solution)/shard_map/ppermute | solution.py:322
  18.6 27.8 %collective-permute-start.6 = (bf16[1024,128]{1,0:T(8,128)(2,1)S(1)}, bf16[1024,128]{1,0:T(8,128)(2,1)S(1)}, u32[]{:S(2)}, u32[]{:S(2)}) collective-permute-start(bf16[1024,128]{1,0:T(8,128)(2,1)S(1)} %get-tuple-element.59), channel_id=1, source_target_pairs={{0,4},{1,5},{2,6},{3,7},{4,0},{5,1},{6,2},{7,3},{8,12},{9,13},{10,... | collective-permute-start | bytes 786440 | tf_op jit(solution)/shard_map/ppermute | solution.py:322
  20.1 36.2 %collective-permute-start.3 = (bf16[1024,128]{1,0:T(8,128)(2,1)S(1)}, bf16[1024,128]{1,0:T(8,128)(2,1)S(1)}, u32[]{:S(2)}, u32[]{:S(2)}) collective-permute-start(bf16[1024,128]{1,0:T(8,128)(2,1)S(1)} %get-tuple-element.51), channel_id=1, source_target_pairs={{0,9},{1,8},{2,11},{3,10},{4,13},{5,12},{6,15},{7,14},{8,1},{9,0},... | collective-permute-start | bytes 786440 | tf_op jit(solution)/shard_map/ppermute | solution.py:322
  20.1 36.2 %collective-permute-start = (bf16[1024,128]{1,0:T(8,128)(2,1)S(1)}, bf16[1024,128]{1,0:T(8,128)(2,1)S(1)}, u32[]{:S(2)}, u32[]{:S(2)}) collective-permute-start(bf16[1024,128]{1,0:T(8,128)(2,1)S(1)} %get-tuple-element.46), channel_id=1, source_target_pairs={{0,5},{1,4},{2,7},{3,6},{4,1},{5,0},{6,3},{7,2},{8,13},{9,12},{10,... | collective-permute-start | bytes 786440 | tf_op jit(solution)/shard_map/ppermute | solution.py:322
  22.7 0.7 copy-start.11
  23.4 35.6 %collective-permute-start.13 = (bf16[1024,128]{1,0:T(8,128)(2,1)S(1)}, bf16[1024,128]{1,0:T(8,128)(2,1)S(1)}, u32[]{:S(2)}, u32[]{:S(2)}) collective-permute-start(bf16[1024,128]{1,0:T(8,128)(2,1)S(1)} %get-tuple-element.76), channel_id=1, source_target_pairs={{0,2},{1,3},{2,0},{3,1},{4,6},{5,7},{6,4},{7,5},{8,10},{9,11},{10,... | collective-permute-start | bytes 786440 | tf_op jit(solution)/shard_map/ppermute | solution.py:322
  45.9 23.5 %collective-permute-start.10 = (bf16[1024,128]{1,0:T(8,128)(2,1)S(1)}, bf16[1024,128]{1,0:T(8,128)(2,1)S(1)}, u32[]{:S(2)}, u32[]{:S(2)}) collective-permute-start(bf16[1024,128]{1,0:T(8,128)(2,1)S(1)} %get-tuple-element.65), channel_id=1, source_target_pairs={{0,10},{1,11},{2,8},{3,9},{4,14},{5,15},{6,12},{7,13},{8,2},{9,3},... | collective-permute-start | bytes 786440 | tf_op jit(solution)/shard_map/ppermute | solution.py:322
  46.4 0.7 copy-start.7
  47.1 22.4 %collective-permute-start.7 = (bf16[1024,128]{1,0:T(8,128)(2,1)S(1)}, bf16[1024,128]{1,0:T(8,128)(2,1)S(1)}, u32[]{:S(2)}, u32[]{:S(2)}) collective-permute-start(bf16[1024,128]{1,0:T(8,128)(2,1)S(1)} %get-tuple-element.60), channel_id=1, source_target_pairs={{0,6},{1,7},{2,4},{3,5},{4,2},{5,3},{6,0},{7,1},{8,14},{9,15},{10,... | collective-permute-start | bytes 786440 | tf_op jit(solution)/shard_map/ppermute | solution.py:322
  56.3 29.0 %collective-permute-start.4 = (bf16[1024,128]{1,0:T(8,128)(2,1)S(1)}, bf16[1024,128]{1,0:T(8,128)(2,1)S(1)}, u32[]{:S(2)}, u32[]{:S(2)}) collective-permute-start(bf16[1024,128]{1,0:T(8,128)(2,1)S(1)} %get-tuple-element.52), channel_id=1, source_target_pairs={{0,11},{1,10},{2,9},{3,8},{4,15},{5,14},{6,13},{7,12},{8,3},{9,2},... | collective-permute-start | bytes 786440 | tf_op jit(solution)/shard_map/ppermute | solution.py:322
  56.3 0.7 copy-start.9
  57.0 30.1 %collective-permute-start.1 = (bf16[1024,128]{1,0:T(8,128)(2,1)S(1)}, bf16[1024,128]{1,0:T(8,128)(2,1)S(1)}, u32[]{:S(2)}, u32[]{:S(2)}) collective-permute-start(bf16[1024,128]{1,0:T(8,128)(2,1)S(1)} %get-tuple-element.47), channel_id=1, source_target_pairs={{0,3},{1,2},{2,1},{3,0},{4,7},{5,6},{6,5},{7,4},{8,11},{9,10},{10,... | collective-permute-start | bytes 786440 | tf_op jit(solution)/shard_map/ppermute | solution.py:322
  59.1 0.7 copy-start.13
  59.8 33.1 %collective-permute-start.14 = (bf16[1024,128]{1,0:T(8,128)(2,1)}, bf16[1024,128]{1,0:T(8,128)(2,1)}, u32[]{:S(2)}, u32[]{:S(2)}) collective-permute-start(bf16[1024,128]{1,0:T(8,128)(2,1)} %get-tuple-element.82), channel_id=1, source_target_pairs={{0,7},{1,6},{2,5},{3,4},{4,3},{5,2},{6,1},{7,0},{8,15},{9,14},{10,... | collective-permute-start | bytes 786440 | tf_op jit(solution)/shard_map/ppermute | solution.py:322
  69.5 47.5 %collective-permute-start.11 = (bf16[1024,128]{1,0:T(8,128)(2,1)}, bf16[1024,128]{1,0:T(8,128)(2,1)S(1)}, u32[]{:S(2)}, u32[]{:S(2)}) collective-permute-start(bf16[1024,128]{1,0:T(8,128)(2,1)} %get-tuple-element.66), channel_id=1, source_target_pairs={{0,13},{1,12},{2,15},{3,14},{4,9},{5,8},{6,11},{7,10},{8,5},{9,4},... | collective-permute-start | bytes 786440 | tf_op jit(solution)/shard_map/ppermute | solution.py:322
  69.5 0.7 copy-start.15
  70.3 46.8 %collective-permute-start.8 = (bf16[1024,128]{1,0:T(8,128)(2,1)}, bf16[1024,128]{1,0:T(8,128)(2,1)S(1)}, u32[]{:S(2)}, u32[]{:S(2)}) collective-permute-start(bf16[1024,128]{1,0:T(8,128)(2,1)} %get-tuple-element.61), channel_id=1, source_target_pairs={{0,12},{1,13},{2,14},{3,15},{4,8},{5,9},{6,10},{7,11},{8,4},{9,5},... | collective-permute-start | bytes 786440 | tf_op jit(solution)/shard_map/ppermute | solution.py:322
  85.3 35.5 %collective-permute-start.5 = (bf16[1024,128]{1,0:T(8,128)(2,1)S(1)}, bf16[1024,128]{1,0:T(8,128)(2,1)S(1)}, u32[]{:S(2)}, u32[]{:S(2)}) collective-permute-start(bf16[1024,128]{1,0:T(8,128)(2,1)S(1)} %get-tuple-element.53), channel_id=1, source_target_pairs={{0,15},{1,14},{2,13},{3,12},{4,11},{5,10},{6,9},{7,8},{8,7},{9,6},... | collective-permute-start | bytes 786440 | tf_op jit(solution)/shard_map/ppermute | solution.py:322
  87.2 0.7 copy-start.17
  87.9 33.0 %collective-permute-start.2 = (bf16[1024,128]{1,0:T(8,128)(2,1)S(1)}, bf16[1024,128]{1,0:T(8,128)(2,1)S(1)}, u32[]{:S(2)}, u32[]{:S(2)}) collective-permute-start(bf16[1024,128]{1,0:T(8,128)(2,1)S(1)} %get-tuple-element.48), channel_id=1, source_target_pairs={{0,14},{1,15},{2,12},{3,13},{4,10},{5,11},{6,8},{7,9},{8,6},{9,7},... | collective-permute-start | bytes 786440 | tf_op jit(solution)/shard_map/ppermute | solution.py:322
  92.9 1.0 copy-start.8
  93.9 0.9 copy-start.10
  94.8 0.9 copy-start.12
  95.8 0.9 copy-start.14
  96.7 0.9 copy-start.16
  97.7 0.9 copy-start.18
  (3 other events, 2.0 us)
where the time goes:
time: 128 us; the launch traced here: 127 us
  waiting for transfers between devices  47.4 us (37%)
  Pallas kernels  35.4 us (28%)
  starting transfers between devices  29.2 us (23%)
  local copies, waits for them, and re-layouts  15 us (12%)
    ppermute x15, waiting for transfers between devices, send(): lax.ppermute(piece, 'work', [(i, i ^ shift) for i in range(workers)])  47.4 us
    pallas_call x4, Pallas kernels, add_group(): pl.pallas_call(functools.partial(group_kernel, first, last, units, per_un...  28.4 us
    ppermute x15, starting transfers between devices, send(): lax.ppermute(piece, 'work', [(i, i ^ shift) for i in range(workers)])  21.8 us
    unnamed x38, local copies, waits for them, and re-layouts  15 us
    all_to_all x1, starting transfers between devices, per_device(): lax.all_to_all(matrices, 'work', split_axis=0, concat_axis=0, tiled=True)  7.38 us
    pallas_call x2, Pallas kernels, choose_pieces(): pl.pallas_call(functools.partial(pieces_kernel, shifts), in_specs=[pl.Blo...  2.87 us
  transfers between devices with their start and end apart: 16, of which 4 were waited for; matrix products, arithmetic and copies ran while one was open for 0% of the time, Pallas kernels for 21%

commit v1 on v0

--- a/solution.py
+++ b/solution.py
@@ -13,9 +13,9 @@
 B_BLOCK = 64
 ACC = jnp.bfloat16
 GROUPS = ((0, 1, 2, 3), (4, 5), (6,), (7,))
-IN_FLIGHT = 5
+IN_FLIGHT = 6
 FAR_TURNS = (2, 4)
-VMEM = 36 * 1024 * 1024
+HELD_BACK = 3
 SMALL_VMEM = 16 * 1024 * 1024
 
 
@@ -286,7 +286,7 @@
         out_shape=out_shape,
         scratch_shapes=scratch,
         compiler_params=pltpu.CompilerParams(
-            dimension_semantics=("arbitrary",), vmem_limit_bytes=VMEM
+            dimension_semantics=("arbitrary",), vmem_limit_bytes=SMALL_VMEM + 4 * extent * extent * (depth + 8)
         ),
         cost_estimate=pl.CostEstimate(
             flops=6 * MOST * rows * extent * extent,
@@ -302,8 +302,8 @@
     per_unit = UNIT_ROWS * workers // extent
     half = workers // 2
     far = list(range(half, workers))
-    near = [s for pair in zip(range(half // 2), range(half // 2, half)) for s in pair][1:]
-    near = [1, *(s for s in near if s != 1)]
+    upper, lower = list(range(half // 2, half)), list(range(2, half // 2))
+    near = [1, *upper[:-1], *lower, upper[-1]]
     order = []
     while far or near:
         take_far = far and (not near or len(order) % IN_FLIGHT in FAR_TURNS)
@@ -326,13 +326,18 @@
     matrices = choose_matrices(perambs, peramb_ids, sink_counts, workers, extent)
     matrices = lax.all_to_all(matrices, "work", split_axis=0, concat_axis=0, tiled=True)
     leg3, leg2, leg1 = make_legs(matrices, sink_counts, weights, workers)
-    for place in range(IN_FLIGHT, len(order)):
+    for place in range(IN_FLIGHT, len(order) - HELD_BACK):
         send(place)
 
     acc = None
     for group, units in enumerate(GROUPS):
         members = [arrived[u * per_unit + lane] for u in units for lane in range(per_unit)]
         acc = add_group(units, members, leg3, leg2, leg1, acc, group == len(GROUPS) - 1)
+        if group == 0:
+            for place in range(len(order) - HELD_BACK, len(order)):
+                shift = order[place]
+                pieces[shift], acc = lax.optimization_barrier((pieces[shift], acc))
+                send(place)
     return acc.reshape(1, extent * extent, extent)
 
 

time: 128 us -> 131 us (1.023)
  the two profiles are of different devices: /device:TPU:0 before, /device:TPU:11 now
where the time goes in v1:
time: 131 us
  waiting for transfers between devices  55.3 us (42%)
  Pallas kernels  35 us (27%)
  starting transfers between devices  30 us (23%)
  local copies, waits for them, and re-layouts  10.1 us (8%)
    ppermute x15, waiting for transfers between devices, send(): lax.ppermute(piece, 'work', [(i, i ^ shift) for i in range(workers)])  55.3 us
    pallas_call x4, Pallas kernels, add_group(): pl.pallas_call(functools.partial(group_kernel, first, last, units, per_un...  28.1 us
    ppermute x15, starting transfers between devices, send(): lax.ppermute(piece, 'work', [(i, i ^ shift) for i in range(workers)])  23.3 us
    unnamed x26, local copies, waits for them, and re-layouts  10.1 us
    all_to_all x1, starting transfers between devices, per_device(): lax.all_to_all(matrices, 'work', split_axis=0, concat_axis=0, tiled=True)  6.61 us
    pallas_call x2, Pallas kernels, choose_pieces(): pl.pallas_call(functools.partial(pieces_kernel, shifts), in_specs=[pl.Blo...  2.87 us
  transfers between devices with their start and end apart: 16, of which 8 were waited for; matrix products, arithmetic and copies ran while one was open for 0% of the time, Pallas kernels for 20%

profile of v1, /device:TPU:11, one launch (start us, length us, event | category | flops | bytes accessed | tf_op | source)
XLA Modules:
  0.0 130.7 jit_solution(1314424802966218854)
XLA Ops:
  0.0 0.9 copy-done.1
  2.3 2.2 %shard_map.66 = bf16[16,144,128]{2,1,0:T(8,128)(2,1)} custom-call(s32[16]{0:T(128)S(1)} %copy-done.4, s32[3,48]{1,0:T(4,128)S(1)} %bitcast.2, bf16[96,1024]{1,0:T(8,128)(2,1)S(1)} %copy-done.1), custom_call_target="tpu_custom_call" | custom-call | tf_op jit(solution)/shard_map/pallas_call | solution.py:89
  4.5 6.6 %all-to-all-start = ((bf16[16,144,128]{2,1,0:T(8,128)(2,1)}), bf16[16,144,128]{2,1,0:T(8,128)(2,1)S(1)}, u32[]{:S(2)}, u32[]{:S(2)}) async-start(bf16[16,144,128]{2,1,0:T(8,128)(2,1)} %shard_map.66), calls=%async_computation | async-start | bytes 1179648 | tf_op jit(solution)/shard_map/all_to_all | solution.py:327
  11.1 2.2 %copy-done = bf16[16,1024,128]{2,1,0:T(8,128)(2,1)S(1)} copy-done((bf16[16,1024,128]{2,1,0:T(8,128)(2,1)S(1)}, bf16[16,1024,128]{2,1,0:T(8,128)(2,1)}, u32[]{:S(2)}) %copy-start) | copy-done | bytes 4194328
  13.9 0.9 shard_map.65
  15.3 1.8 %collective-permute-start.4 = (bf16[1024,128]{1,0:T(8,128)(2,1)S(1)}, bf16[1024,128]{1,0:T(8,128)(2,1)S(1)}, u32[]{:S(2)}, u32[]{:S(2)}) collective-permute-start(bf16[1024,128]{1,0:T(8,128)(2,1)S(1)} %get-tuple-element.58), channel_id=1, source_target_pairs={{0,5},{1,4},{2,7},{3,6},{4,1},{5,0},{6,3},{7,2},{8,13},{9,12},{10,... | collective-permute-start | bytes 786440 | tf_op jit(solution)/shard_map/ppermute | solution.py:322
  17.1 1.2 collective-permute-start.5
  18.3 2.1 %collective-permute-start.8 = (bf16[1024,128]{1,0:T(8,128)(2,1)S(1)}, bf16[1024,128]{1,0:T(8,128)(2,1)S(1)}, u32[]{:S(2)}, u32[]{:S(2)}) collective-permute-start(bf16[1024,128]{1,0:T(8,128)(2,1)S(1)} %get-tuple-element.74), channel_id=1, source_target_pairs={{0,8},{1,9},{2,10},{3,11},{4,12},{5,13},{6,14},{7,15},{8,0},{9,1},... | collective-permute-start | bytes 786440 | tf_op jit(solution)/shard_map/ppermute | solution.py:322
  20.3 1.9 %shard_map.64 = (bf16[1024,128]{1,0:T(8,128)(2,1)S(1)}, bf16[1024,128]{1,0:T(8,128)(2,1)}, bf16[1024,128]{1,0:T(8,128)(2,1)}, bf16[1024,128]{1,0:T(8,128)(2,1)},...) custom-call(s32[16]{0:T(128)S(1)} %copy-done.3, ...), custom_call_target="tpu_custom_call" | custom-call | tf_op jit(solution)/shard_map/pallas_call | solution.py:42
  23.0 0.8 collective-permute-start.13
  23.8 13.8 %collective-permute-done.2.refs_4_ = bf16[1024,128]{1,0:T(8,128)(2,1)S(1)} collective-permute-done((bf16[1024,128]{1,0:T(8,128)(2,1)S(1)}, bf16[1024,128]{1,0:T(8,128)(2,1)S(1)}, u32[]{:S(2)}, u32[]{:S(2)}) %collective-permute-start.2) | collective-permute-done | bytes 262176 | tf_op jit(solution)/shard_map/ppermute | solution.py:322
  37.7 1.2 collective-permute-start.1
  38.8 4.4 %collective-permute-done.4.refs_5_ = bf16[1024,128]{1,0:T(8,128)(2,1)S(1)} collective-permute-done((bf16[1024,128]{1,0:T(8,128)(2,1)S(1)}, bf16[1024,128]{1,0:T(8,128)(2,1)S(1)}, u32[]{:S(2)}, u32[]{:S(2)}) %collective-permute-start.4) | collective-permute-done | bytes 262176 | tf_op jit(solution)/shard_map/ppermute | solution.py:322
  44.0 2.4 %collective-permute-start.3 = (bf16[1024,128]{1,0:T(8,128)(2,1)}, bf16[1024,128]{1,0:T(8,128)(2,1)}, u32[]{:S(2)}, u32[]{:S(2)}) collective-permute-start(bf16[1024,128]{1,0:T(8,128)(2,1)} %get-tuple-element.55), channel_id=1, source_target_pairs={{0,3},{1,2},{2,1},{3,0},{4,7},{5,6},{6,5},{7,4},{8,11},{9,10},{10,... | collective-permute-start | bytes 786440 | tf_op jit(solution)/shard_map/ppermute | solution.py:322
  46.4 2.5 %collective-permute-done.5.refs_6_ = bf16[1024,128]{1,0:T(8,128)(2,1)S(1)} collective-permute-done((bf16[1024,128]{1,0:T(8,128)(2,1)S(1)}, bf16[1024,128]{1,0:T(8,128)(2,1)S(1)}, u32[]{:S(2)}, u32[]{:S(2)}) %collective-permute-start.5) | collective-permute-done | bytes 262176 | tf_op jit(solution)/shard_map/ppermute | solution.py:322
  49.7 3.9 %collective-permute-start.6 = (bf16[1024,128]{1,0:T(8,128)(2,1)}, bf16[1024,128]{1,0:T(8,128)(2,1)}, u32[]{:S(2)}, u32[]{:S(2)}) collective-permute-start(bf16[1024,128]{1,0:T(8,128)(2,1)} %get-tuple-element.63), channel_id=1, source_target_pairs={{0,7},{1,6},{2,5},{3,4},{4,3},{5,2},{6,1},{7,0},{8,15},{9,14},{10,... | collective-permute-start | bytes 786440 | tf_op jit(solution)/shard_map/ppermute | solution.py:322
  54.9 1.9 %shard_map.67 = (bf16[128,768]{1,0:T(8,128)(2,1)S(1)}, bf16[768,128]{1,0:T(8,128)(2,1)S(1)}, bf16[8,96,128]{2,1,0:T(8,128)(2,1)S(1)}) custom-call(s32[16]{0:T(128)S(1)} %copy-done.5, f32[48]{0:T(128)S(1)} %copy-done.6, bf16[16,144,128]{2,1,0:T(8,128)(2,1)S(1)} %all-to-all-done.matrix_ref), custom_call_target="tpu_custom_call" | custom-call | tf_op jit(solution)/shard_map/pallas_call | solution.py:145
  56.7 4.6 %collective-permute-start.14 = (bf16[1024,128]{1,0:T(8,128)(2,1)S(1)}, bf16[1024,128]{1,0:T(8,128)(2,1)S(1)}, u32[]{:S(2)}, u32[]{:S(2)}) collective-permute-start(bf16[1024,128]{1,0:T(8,128)(2,1)S(1)} %get-tuple-element.85), channel_id=1, source_target_pairs={{0,11},{1,10},{2,9},{3,8},{4,15},{5,14},{6,13},{7,12},{8,3},{9,2},... | collective-permute-start | bytes 786440 | tf_op jit(solution)/shard_map/ppermute | solution.py:322
  61.4 3.1 %collective-permute-done.6.refs_7_ = bf16[1024,128]{1,0:T(8,128)(2,1)} collective-permute-done((bf16[1024,128]{1,0:T(8,128)(2,1)}, bf16[1024,128]{1,0:T(8,128)(2,1)}, u32[]{:S(2)}, u32[]{:S(2)}) %collective-permute-start.6) | collective-permute-done | bytes 262176 | tf_op jit(solution)/shard_map/ppermute | solution.py:322
  64.4 0.9 copy-done.8
  65.4 0.9 copy-done.10
  66.3 0.9 copy-done.12
  67.3 11.9 %shard_map.68.refs_7_ = bf16[128,128,128]{2,1,0:T(8,128)(2,1)S(1)} custom-call(bf16[1024,128]{1,0:T(8,128)(2,1)S(1)} %copy-done.12, bf16[1024,128]{1,0:T(8,128)(2,1)S(1)} %collective-permute-done.refs_1_, bf16[1024,128]{1,0:T(8,128)(2,1)} %collective-permute-done.1.refs_2_, bf16[1024,128]{1,0:T(8,128)(2,1)} %collective-permute-done.3.refs_3_, ...), custom_call_target="tpu_custom_call" | custom-call | flops 4831838208 | bytes 25165824 | tf_op jit(solution)/shard_map/pallas_call | solution.py:281
  79.2 1.7 %collective-permute-start.12 = (bf16[1024,128]{1,0:T(8,128)(2,1)S(1)}, bf16[1024,128]{1,0:T(8,128)(2,1)S(1)}, u32[]{:S(2)}, u32[]{:S(2)}) collective-permute-start(bf16[1024,128]{1,0:T(8,128)(2,1)S(1)} %get-tuple-element.79), channel_id=1, source_target_pairs={{0,13},{1,12},{2,15},{3,14},{4,9},{5,8},{6,11},{7,10},{8,5},{9,4},... | collective-permute-start | bytes 786440 | tf_op jit(solution)/shard_map/ppermute | solution.py:322
  81.2 1.7 %collective-permute-start.10 = (bf16[1024,128]{1,0:T(8,128)(2,1)S(1)}, bf16[1024,128]{1,0:T(8,128)(2,1)S(1)}, u32[]{:S(2)}, u32[]{:S(2)}) collective-permute-start(bf16[1024,128]{1,0:T(8,128)(2,1)S(1)} %get-tuple-element.76), channel_id=1, source_target_pairs={{0,15},{1,14},{2,13},{3,12},{4,11},{5,10},{6,9},{7,8},{8,7},{9,6},... | collective-permute-start | bytes 786440 | tf_op jit(solution)/shard_map/ppermute | solution.py:322
  82.9 21.6 %collective-permute-done.14.refs_3_ = bf16[1024,128]{1,0:T(8,128)(2,1)S(1)} collective-permute-done((bf16[1024,128]{1,0:T(8,128)(2,1)S(1)}, bf16[1024,128]{1,0:T(8,128)(2,1)S(1)}, u32[]{:S(2)}, u32[]{:S(2)}) %collective-permute-start.14) | collective-permute-done | bytes 262176 | tf_op jit(solution)/shard_map/ppermute | solution.py:322
  104.5 6.1 %shard_map.69.refs_5_ = bf16[128,128,128]{2,1,0:T(8,128)(2,1)S(1)} custom-call(bf16[1024,128]{1,0:T(8,128)(2,1)S(1)} %collective-permute-done.8.refs_0_, bf16[1024,128]{1,0:T(8,128)(2,1)S(1)} %collective-permute-done.13.refs_1_, bf16[1024,128]{1,0:T(8,128)(2,1)S(1)} %collective-permute-done.9.refs_2_, bf16[1024,128]{1,0:T(8,128)(2,1)S(1)} %collective-permute-done.14.refs_3_, ...), custom_call_target="tpu_custom_call" | custom-call | flops 2415919104 | bytes 25165824 | tf_op jit(solution)/shard_map/pallas_call | solution.py:281
  110.6 2.0 %collective-permute-done.12.refs_1_ = bf16[1024,128]{1,0:T(8,128)(2,1)S(1)} collective-permute-done((bf16[1024,128]{1,0:T(8,128)(2,1)S(1)}, bf16[1024,128]{1,0:T(8,128)(2,1)S(1)}, u32[]{:S(2)}, u32[]{:S(2)}) %collective-permute-start.12) | collective-permute-done | bytes 262176 | tf_op jit(solution)/shard_map/ppermute | solution.py:322
  112.7 3.8 %shard_map.70.refs_5_ = bf16[128,128,128]{2,1,0:T(8,128)(2,1)S(1)} custom-call(bf16[1024,128]{1,0:T(8,128)(2,1)S(1)} %collective-permute-done.11.refs_0_, bf16[1024,128]{1,0:T(8,128)(2,1)S(1)} %collective-permute-done.12.refs_1_, bf16[128,768]{1,0:T(8,128)(2,1)S(1)} %get-tuple-element.64.refs_8_.refs_4_.refs_2_, ...), custom_call_target="tpu_custom_call" | custom-call | flops 1207959552 | bytes 25165824 | tf_op jit(solution)/shard_map/pallas_call | solution.py:281
  116.5 2.0 %collective-permute-done.7.refs_0_ = bf16[1024,128]{1,0:T(8,128)(2,1)S(1)} collective-permute-done((bf16[1024,128]{1,0:T(8,128)(2,1)S(1)}, bf16[1024,128]{1,0:T(8,128)(2,1)S(1)}, u32[]{:S(2)}, u32[]{:S(2)}) %collective-permute-start.7) | collective-permute-done | bytes 262176 | tf_op jit(solution)/shard_map/ppermute | solution.py:322
  118.5 5.8 %collective-permute-done.10.refs_1_ = bf16[1024,128]{1,0:T(8,128)(2,1)S(1)} collective-permute-done((bf16[1024,128]{1,0:T(8,128)(2,1)S(1)}, bf16[1024,128]{1,0:T(8,128)(2,1)S(1)}, u32[]{:S(2)}, u32[]{:S(2)}) %collective-permute-start.10) | collective-permute-done | bytes 262176 | tf_op jit(solution)/shard_map/ppermute | solution.py:322
  124.3 6.2 %shard_map.71 = bf16[128,128,128]{2,1,0:T(8,128)(2,1)} custom-call(bf16[1024,128]{1,0:T(8,128)(2,1)S(1)} %collective-permute-done.7.refs_0_, bf16[1024,128]{1,0:T(8,128)(2,1)S(1)} %collective-permute-done.10.refs_1_, bf16[128,768]{1,0:T(8,128)(2,1)S(1)} %get-tuple-element.64.refs_8_.refs_4_.refs_2_, ...), custom_call_target="tpu_custom_call" | custom-call | flops 1207959552 | bytes 25165824 | tf_op jit(solution)/shard_map/pallas_call | solution.py:281
  (34 shorter events, 6.2 us)
Async XLA Ops:
  0.0 0.9 copy-start.1
  0.9 0.7 copy-start.2
  1.6 0.7 copy-start.4
  4.5 50.4 %all-to-all-start = ((bf16[16,144,128]{2,1,0:T(8,128)(2,1)}), bf16[16,144,128]{2,1,0:T(8,128)(2,1)S(1)}, u32[]{:S(2)}, u32[]{:S(2)}) async-start(bf16[16,144,128]{2,1,0:T(8,128)(2,1)} %shard_map.66), calls=%async_computation | async-start | bytes 1179648 | tf_op jit(solution)/shard_map/all_to_all | solution.py:327
  11.1 2.2 %copy-start = (bf16[16,1024,128]{2,1,0:T(8,128)(2,1)S(1)}, bf16[16,1024,128]{2,1,0:T(8,128)(2,1)}, u32[]{:S(2)}) copy-start(bf16[16,1024,128]{2,1,0:T(8,128)(2,1)} %source_ref.3) | copy-start | bytes 12582916
  13.3 0.7 copy-start.3
  13.9 40.9 %copy-start.5 = (s32[16]{0:T(128)S(1)}, s32[16]{0:T(128)}, u32[]{:S(2)}) copy-start(s32[16]{0:T(128)} %counts_ref.3) | copy-start | bytes 196
  13.9 40.9 %copy-start.6 = (f32[48]{0:T(128)S(1)}, f32[48]{0:T(128)}, u32[]{:S(2)}) copy-start(f32[48]{0:T(128)} %weights_ref.1) | copy-start | bytes 580
  14.9 8.2 %collective-permute-start = (bf16[1024,128]{1,0:T(8,128)(2,1)S(1)}, bf16[1024,128]{1,0:T(8,128)(2,1)S(1)}, u32[]{:S(2)}, u32[]{:S(2)}) collective-permute-start(bf16[1024,128]{1,0:T(8,128)(2,1)S(1)} %get-tuple-element.50), channel_id=1, source_target_pairs={{0,1},{1,0},{2,3},{3,2},{4,5},{5,4},{6,7},{7,6},{8,9},{9,8},{10,11... | collective-permute-start | bytes 786440 | tf_op jit(solution)/shard_map/ppermute | solution.py:322
  15.3 22.4 %collective-permute-start.2 = (bf16[1024,128]{1,0:T(8,128)(2,1)S(1)}, bf16[1024,128]{1,0:T(8,128)(2,1)S(1)}, u32[]{:S(2)}, u32[]{:S(2)}) collective-permute-start(bf16[1024,128]{1,0:T(8,128)(2,1)S(1)} %get-tuple-element.54), channel_id=1, source_target_pairs={{0,4},{1,5},{2,6},{3,7},{4,0},{5,1},{6,2},{7,3},{8,12},{9,13},{10,... | collective-permute-start | bytes 786440 | tf_op jit(solution)/shard_map/ppermute | solution.py:322
  15.3 28.0 %collective-permute-start.4 = (bf16[1024,128]{1,0:T(8,128)(2,1)S(1)}, bf16[1024,128]{1,0:T(8,128)(2,1)S(1)}, u32[]{:S(2)}, u32[]{:S(2)}) collective-permute-start(bf16[1024,128]{1,0:T(8,128)(2,1)S(1)} %get-tuple-element.58), channel_id=1, source_target_pairs={{0,5},{1,4},{2,7},{3,6},{4,1},{5,0},{6,3},{7,2},{8,13},{9,12},{10,... | collective-permute-start | bytes 786440 | tf_op jit(solution)/shard_map/ppermute | solution.py:322
  17.1 31.8 %collective-permute-start.5 = (bf16[1024,128]{1,0:T(8,128)(2,1)S(1)}, bf16[1024,128]{1,0:T(8,128)(2,1)S(1)}, u32[]{:S(2)}, u32[]{:S(2)}) collective-permute-start(bf16[1024,128]{1,0:T(8,128)(2,1)S(1)} %get-tuple-element.61), channel_id=1, source_target_pairs={{0,6},{1,7},{2,4},{3,5},{4,2},{5,3},{6,0},{7,1},{8,14},{9,15},{10,... | collective-permute-start | bytes 786440 | tf_op jit(solution)/shard_map/ppermute | solution.py:322
  18.3 35.3 %collective-permute-start.8 = (bf16[1024,128]{1,0:T(8,128)(2,1)S(1)}, bf16[1024,128]{1,0:T(8,128)(2,1)S(1)}, u32[]{:S(2)}, u32[]{:S(2)}) collective-permute-start(bf16[1024,128]{1,0:T(8,128)(2,1)S(1)} %get-tuple-element.74), channel_id=1, source_target_pairs={{0,8},{1,9},{2,10},{3,11},{4,12},{5,13},{6,14},{7,15},{8,0},{9,1},... | collective-permute-start | bytes 786440 | tf_op jit(solution)/shard_map/ppermute | solution.py:322
  22.3 0.7 copy-start.11
  23.0 31.1 %collective-permute-start.13 = (bf16[1024,128]{1,0:T(8,128)(2,1)S(1)}, bf16[1024,128]{1,0:T(8,128)(2,1)S(1)}, u32[]{:S(2)}, u32[]{:S(2)}) collective-permute-start(bf16[1024,128]{1,0:T(8,128)(2,1)S(1)} %get-tuple-element.82), channel_id=1, source_target_pairs={{0,9},{1,8},{2,11},{3,10},{4,13},{5,12},{6,15},{7,14},{8,1},{9,0},... | collective-permute-start | bytes 786440 | tf_op jit(solution)/shard_map/ppermute | solution.py:322
  37.7 19.1 %collective-permute-start.1 = (bf16[1024,128]{1,0:T(8,128)(2,1)}, bf16[1024,128]{1,0:T(8,128)(2,1)}, u32[]{:S(2)}, u32[]{:S(2)}) collective-permute-start(bf16[1024,128]{1,0:T(8,128)(2,1)} %get-tuple-element.52), channel_id=1, source_target_pairs={{0,2},{1,3},{2,0},{3,1},{4,6},{5,7},{6,4},{7,5},{8,10},{9,11},{10,... | collective-permute-start | bytes 786440 | tf_op jit(solution)/shard_map/ppermute | solution.py:322
  43.3 0.7 copy-start.7
  44.0 17.4 %collective-permute-start.3 = (bf16[1024,128]{1,0:T(8,128)(2,1)}, bf16[1024,128]{1,0:T(8,128)(2,1)}, u32[]{:S(2)}, u32[]{:S(2)}) collective-permute-start(bf16[1024,128]{1,0:T(8,128)(2,1)} %get-tuple-element.55), channel_id=1, source_target_pairs={{0,3},{1,2},{2,1},{3,0},{4,7},{5,6},{6,5},{7,4},{8,11},{9,10},{10,... | collective-permute-start | bytes 786440 | tf_op jit(solution)/shard_map/ppermute | solution.py:322
  48.9 0.7 copy-start.9
  49.7 14.8 %collective-permute-start.6 = (bf16[1024,128]{1,0:T(8,128)(2,1)}, bf16[1024,128]{1,0:T(8,128)(2,1)}, u32[]{:S(2)}, u32[]{:S(2)}) collective-permute-start(bf16[1024,128]{1,0:T(8,128)(2,1)} %get-tuple-element.63), channel_id=1, source_target_pairs={{0,7},{1,6},{2,5},{3,4},{4,3},{5,2},{6,1},{7,0},{8,15},{9,14},{10,... | collective-permute-start | bytes 786440 | tf_op jit(solution)/shard_map/ppermute | solution.py:322
  53.6 27.6 %collective-permute-start.9 = (bf16[1024,128]{1,0:T(8,128)(2,1)}, bf16[1024,128]{1,0:T(8,128)(2,1)S(1)}, u32[]{:S(2)}, u32[]{:S(2)}) collective-permute-start(bf16[1024,128]{1,0:T(8,128)(2,1)} %get-tuple-element.75), channel_id=1, source_target_pairs={{0,10},{1,11},{2,8},{3,9},{4,14},{5,15},{6,12},{7,13},{8,2},{9,3},... | collective-permute-start | bytes 786440 | tf_op jit(solution)/shard_map/ppermute | solution.py:322
  54.1 56.6 %collective-permute-start.11 = (bf16[1024,128]{1,0:T(8,128)(2,1)S(1)}, bf16[1024,128]{1,0:T(8,128)(2,1)S(1)}, u32[]{:S(2)}, u32[]{:S(2)}) collective-permute-start(bf16[1024,128]{1,0:T(8,128)(2,1)S(1)} %get-tuple-element.77), channel_id=1, source_target_pairs={{0,12},{1,13},{2,14},{3,15},{4,8},{5,9},{6,10},{7,11},{8,4},{9,5},... | collective-permute-start | bytes 786440 | tf_op jit(solution)/shard_map/ppermute | solution.py:322
  56.7 47.7 %collective-permute-start.14 = (bf16[1024,128]{1,0:T(8,128)(2,1)S(1)}, bf16[1024,128]{1,0:T(8,128)(2,1)S(1)}, u32[]{:S(2)}, u32[]{:S(2)}) collective-permute-start(bf16[1024,128]{1,0:T(8,128)(2,1)S(1)} %get-tuple-element.85), channel_id=1, source_target_pairs={{0,11},{1,10},{2,9},{3,8},{4,15},{5,14},{6,13},{7,12},{8,3},{9,2},... | collective-permute-start | bytes 786440 | tf_op jit(solution)/shard_map/ppermute | solution.py:322
  64.4 0.9 copy-start.8
  65.4 0.9 copy-start.10
  66.3 0.9 copy-start.12
  79.2 33.4 %collective-permute-start.12 = (bf16[1024,128]{1,0:T(8,128)(2,1)S(1)}, bf16[1024,128]{1,0:T(8,128)(2,1)S(1)}, u32[]{:S(2)}, u32[]{:S(2)}) collective-permute-start(bf16[1024,128]{1,0:T(8,128)(2,1)S(1)} %get-tuple-element.79), channel_id=1, source_target_pairs={{0,13},{1,12},{2,15},{3,14},{4,9},{5,8},{6,11},{7,10},{8,5},{9,4},... | collective-permute-start | bytes 786440 | tf_op jit(solution)/shard_map/ppermute | solution.py:322
  80.9 37.6 %collective-permute-start.7 = (bf16[1024,128]{1,0:T(8,128)(2,1)S(1)}, bf16[1024,128]{1,0:T(8,128)(2,1)S(1)}, u32[]{:S(2)}, u32[]{:S(2)}) collective-permute-start(bf16[1024,128]{1,0:T(8,128)(2,1)S(1)} %get-tuple-element.69), channel_id=1, source_target_pairs={{0,14},{1,15},{2,12},{3,13},{4,10},{5,11},{6,8},{7,9},{8,6},{9,7},... | collective-permute-start | bytes 786440 | tf_op jit(solution)/shard_map/ppermute | solution.py:322
  81.2 43.1 %collective-permute-start.10 = (bf16[1024,128]{1,0:T(8,128)(2,1)S(1)}, bf16[1024,128]{1,0:T(8,128)(2,1)S(1)}, u32[]{:S(2)}, u32[]{:S(2)}) collective-permute-start(bf16[1024,128]{1,0:T(8,128)(2,1)S(1)} %get-tuple-element.76), channel_id=1, source_target_pairs={{0,15},{1,14},{2,13},{3,12},{4,11},{5,10},{6,9},{7,8},{8,7},{9,6},... | collective-permute-start | bytes 786440 | tf_op jit(solution)/shard_map/ppermute | solution.py:322

commit v2 on v1

--- a/solution.py
+++ b/solution.py
@@ -12,11 +12,12 @@
 UNIT_ROWS = 16
 B_BLOCK = 64
 ACC = jnp.bfloat16
-GROUPS = ((0, 1, 2, 3), (4, 5), (6,), (7,))
-IN_FLIGHT = 6
-FAR_TURNS = (2, 4)
-HELD_BACK = 3
+GROUPS = ((0, 2, 4), (3, 5), (1, 6), (7,))
+IN_FLIGHT = 5
+FAR_TURNS = (2, 4, 6, 8)
+HELD_BACK = 5
 SMALL_VMEM = 16 * 1024 * 1024
+ROOM = 13 * 1024 * 1024
 
 
 def pieces_kernel(shifts, ids_ref, source_ref, *refs):
@@ -286,7 +287,7 @@
         out_shape=out_shape,
         scratch_shapes=scratch,
         compiler_params=pltpu.CompilerParams(
-            dimension_semantics=("arbitrary",), vmem_limit_bytes=SMALL_VMEM + 4 * extent * extent * (depth + 8)
+            dimension_semantics=("arbitrary",), vmem_limit_bytes=ROOM + 4 * extent * extent * (depth + 8)
         ),
         cost_estimate=pl.CostEstimate(
             flops=6 * MOST * rows * extent * extent,
@@ -302,11 +303,10 @@
     per_unit = UNIT_ROWS * workers // extent
     half = workers // 2
     far = list(range(half, workers))
-    upper, lower = list(range(half // 2, half)), list(range(2, half // 2))
-    near = [1, *upper[:-1], *lower, upper[-1]]
+    near = [1, *range(half // 2, half), *range(2, half // 2)]
     order = []
     while far or near:
-        take_far = far and (not near or len(order) % IN_FLIGHT in FAR_TURNS)
+        take_far = far and (not near or len(order) in FAR_TURNS)
         order.append(far.pop(0) if take_far else near.pop(0))
     early, late = tuple(order[:IN_FLIGHT]), (0, *order[IN_FLIGHT:])
     pieces = dict(zip(early, choose_pieces(sources, source_ids, early)))

time: 131 us -> 129 us (0.985)
  local copies, waits for them, and re-layouts: 10.1 us -> 15 us
  waiting for transfers between devices: 55.3 us -> 51.5 us
  starting transfers between devices: 30 us -> 26.6 us
    unnamed x26 -> x38, local copies, waits for them, and re-layouts: 10.1 us -> 15 us
    ppermute x15, waiting for transfers between devices: 55.3 us -> 51.5 us  [send(): lax.ppermute(piece, 'work', [(i, i ^ shift) for i in range(workers)])]
    ppermute x15, starting transfers between devices: 23.3 us -> 20 us  [send(): lax.ppermute(piece, 'work', [(i, i ^ shift) for i in range(workers)])]
  transfers between devices with their start and end apart: 16 -> 16, of which waited for: 8 -> 8; matrix products, arithmetic and copies ran while one was open for 0% -> 0% of each run, Pallas kernels for 20% -> 21%
where the time goes in v2:
time: 129 us; the launch traced here: 128 us
  waiting for transfers between devices  51.5 us (40%)
  Pallas kernels  34.9 us (27%)
  starting transfers between devices  26.6 us (21%)
  local copies, waits for them, and re-layouts  15 us (12%)
    ppermute x15, waiting for transfers between devices, send(): lax.ppermute(piece, 'work', [(i, i ^ shift) for i in range(workers)])  51.5 us
    pallas_call x4, Pallas kernels, add_group(): pl.pallas_call(functools.partial(group_kernel, first, last, units, per_un...  28.1 us
    ppermute x15, starting transfers between devices, send(): lax.ppermute(piece, 'work', [(i, i ^ shift) for i in range(workers)])  20 us
    unnamed x38, local copies, waits for them, and re-layouts  15 us
    all_to_all x1, starting transfers between devices, per_device(): lax.all_to_all(matrices, 'work', split_axis=0, concat_axis=0, tiled=True)  6.61 us
    pallas_call x2, Pallas kernels, choose_pieces(): pl.pallas_call(functools.partial(pieces_kernel, shifts), in_specs=[pl.Blo...  2.84 us
  transfers between devices with their start and end apart: 16, of which 8 were waited for; matrix products, arithmetic and copies ran while one was open for 0% of the time, Pallas kernels for 21%

profile of v2, /device:TPU:11, one launch (start us, length us, event | category | flops | bytes accessed | tf_op | source)
XLA Modules:
  0.0 128.3 jit_solution(8249779059055268408)
XLA Ops:
  0.0 0.9 copy-done.1
  2.3 2.2 %shard_map.66 = bf16[16,144,128]{2,1,0:T(8,128)(2,1)} custom-call(s32[16]{0:T(128)S(1)} %copy-done.4, s32[3,48]{1,0:T(4,128)S(1)} %bitcast.2, bf16[96,1024]{1,0:T(8,128)(2,1)S(1)} %copy-done.1), custom_call_target="tpu_custom_call" | custom-call | tf_op jit(solution)/shard_map/pallas_call | solution.py:90
  4.5 6.6 %all-to-all-start = ((bf16[16,144,128]{2,1,0:T(8,128)(2,1)}), bf16[16,144,128]{2,1,0:T(8,128)(2,1)S(1)}, u32[]{:S(2)}, u32[]{:S(2)}) async-start(bf16[16,144,128]{2,1,0:T(8,128)(2,1)} %shard_map.66), calls=%async_computation | async-start | bytes 1179648 | tf_op jit(solution)/shard_map/all_to_all | solution.py:327
  11.1 2.2 %copy-done = bf16[16,1024,128]{2,1,0:T(8,128)(2,1)S(1)} copy-done((bf16[16,1024,128]{2,1,0:T(8,128)(2,1)S(1)}, bf16[16,1024,128]{2,1,0:T(8,128)(2,1)}, u32[]{:S(2)}) %copy-start) | copy-done | bytes 4194328
  13.9 0.9 shard_map.65
  15.2 1.8 %collective-permute-start.2 = (bf16[1024,128]{1,0:T(8,128)(2,1)S(1)}, bf16[1024,128]{1,0:T(8,128)(2,1)S(1)}, u32[]{:S(2)}, u32[]{:S(2)}) collective-permute-start(bf16[1024,128]{1,0:T(8,128)(2,1)S(1)} %get-tuple-element.66), channel_id=1, source_target_pairs={{0,5},{1,4},{2,7},{3,6},{4,1},{5,0},{6,3},{7,2},{8,13},{9,12},{10,... | collective-permute-start | bytes 786440 | tf_op jit(solution)/shard_map/ppermute | solution.py:322
  17.0 2.1 %collective-permute-start.3 = (bf16[1024,128]{1,0:T(8,128)(2,1)S(1)}, bf16[1024,128]{1,0:T(8,128)(2,1)S(1)}, u32[]{:S(2)}, u32[]{:S(2)}) collective-permute-start(bf16[1024,128]{1,0:T(8,128)(2,1)S(1)} %get-tuple-element.69), channel_id=1, source_target_pairs={{0,8},{1,9},{2,10},{3,11},{4,12},{5,13},{6,14},{7,15},{8,0},{9,1},... | collective-permute-start | bytes 786440 | tf_op jit(solution)/shard_map/ppermute | solution.py:322
  19.6 2.0 %shard_map.64 = (bf16[1024,128]{1,0:T(8,128)(2,1)S(1)}, bf16[1024,128]{1,0:T(8,128)(2,1)}, bf16[1024,128]{1,0:T(8,128)(2,1)}, bf16[1024,128]{1,0:T(8,128)(2,1)},...) custom-call(s32[16]{0:T(128)S(1)} %copy-done.3, ...), custom_call_target="tpu_custom_call" | custom-call | tf_op jit(solution)/shard_map/pallas_call | solution.py:43
  23.0 12.4 %collective-permute-done.1.refs_2_ = bf16[1024,128]{1,0:T(8,128)(2,1)S(1)} collective-permute-done((bf16[1024,128]{1,0:T(8,128)(2,1)S(1)}, bf16[1024,128]{1,0:T(8,128)(2,1)S(1)}, u32[]{:S(2)}, u32[]{:S(2)}) %collective-permute-start.1) | collective-permute-done | bytes 262176 | tf_op jit(solution)/shard_map/ppermute | solution.py:322
  36.1 5.1 %collective-permute-done.2.refs_3_ = bf16[1024,128]{1,0:T(8,128)(2,1)S(1)} collective-permute-done((bf16[1024,128]{1,0:T(8,128)(2,1)S(1)}, bf16[1024,128]{1,0:T(8,128)(2,1)S(1)}, u32[]{:S(2)}, u32[]{:S(2)}) %collective-permute-start.2) | collective-permute-done | bytes 262176 | tf_op jit(solution)/shard_map/ppermute | solution.py:322
  42.6 4.0 %collective-permute-done.4.refs_5_ = bf16[1024,128]{1,0:T(8,128)(2,1)S(1)} collective-permute-done((bf16[1024,128]{1,0:T(8,128)(2,1)S(1)}, bf16[1024,128]{1,0:T(8,128)(2,1)S(1)}, u32[]{:S(2)}, u32[]{:S(2)}) %collective-permute-start.4) | collective-permute-done | bytes 262176 | tf_op jit(solution)/shard_map/ppermute | solution.py:322
  47.3 4.2 %collective-permute-start.5 = (bf16[1024,128]{1,0:T(8,128)(2,1)}, bf16[1024,128]{1,0:T(8,128)(2,1)S(1)}, u32[]{:S(2)}, u32[]{:S(2)}) collective-permute-start(bf16[1024,128]{1,0:T(8,128)(2,1)} %get-tuple-element.81), channel_id=1, source_target_pairs={{0,11},{1,10},{2,9},{3,8},{4,15},{5,14},{6,13},{7,12},{8,3},{9,2},... | collective-permute-start | bytes 786440 | tf_op jit(solution)/shard_map/ppermute | solution.py:322
  52.5 2.6 %collective-permute-start.11 = (bf16[1024,128]{1,0:T(8,128)(2,1)}, bf16[1024,128]{1,0:T(8,128)(2,1)S(1)}, u32[]{:S(2)}, u32[]{:S(2)}) collective-permute-start(bf16[1024,128]{1,0:T(8,128)(2,1)} %get-tuple-element.93), channel_id=1, source_target_pairs={{0,10},{1,11},{2,8},{3,9},{4,14},{5,15},{6,12},{7,13},{8,2},{9,3},... | collective-permute-start | bytes 786440 | tf_op jit(solution)/shard_map/ppermute | solution.py:322
  55.8 1.7 %shard_map.67 = (bf16[128,768]{1,0:T(8,128)(2,1)S(1)}, bf16[768,128]{1,0:T(8,128)(2,1)S(1)}, bf16[8,96,128]{2,1,0:T(8,128)(2,1)S(1)}) custom-call(s32[16]{0:T(128)S(1)} %copy-done.5, f32[48]{0:T(128)S(1)} %copy-done.6, bf16[16,144,128]{2,1,0:T(8,128)(2,1)S(1)} %all-to-all-done.matrix_ref), custom_call_target="tpu_custom_call" | custom-call | tf_op jit(solution)/shard_map/pallas_call | solution.py:146
  57.5 0.9 copy-done.8
  58.5 0.9 copy-done.10
  59.4 0.9 copy-done.12
  60.4 0.9 copy-done.14
  61.3 0.9 copy-done.16
  62.3 0.9 copy-done.18
  63.2 9.6 %shard_map.68.refs_7_ = bf16[128,128,128]{2,1,0:T(8,128)(2,1)S(1)} custom-call(bf16[1024,128]{1,0:T(8,128)(2,1)S(1)} %copy-done.18, bf16[1024,128]{1,0:T(8,128)(2,1)S(1)} %copy-done.8, bf16[1024,128]{1,0:T(8,128)(2,1)S(1)} %copy-done.10, bf16[1024,128]{1,0:T(8,128)(2,1)S(1)} %copy-done.12, bf16[1024,128]{1,0:T(8,128)(2,1)S(1)} %copy-done.14, ...), custom_call_target="tpu_custom_call" | custom-call | flops 3623878656 | bytes 25165824 | tf_op jit(solution)/shard_map/pallas_call | solution.py:282
  72.9 1.6 %collective-permute-start.10 = (bf16[1024,128]{1,0:T(8,128)(2,1)S(1)}, bf16[1024,128]{1,0:T(8,128)(2,1)S(1)}, u32[]{:S(2)}, u32[]{:S(2)}) collective-permute-start(bf16[1024,128]{1,0:T(8,128)(2,1)S(1)} %get-tuple-element.91), channel_id=1, source_target_pairs={{0,3},{1,2},{2,1},{3,0},{4,7},{5,6},{6,5},{7,4},{8,11},{9,10},{10,... | collective-permute-start | bytes 786440 | tf_op jit(solution)/shard_map/ppermute | solution.py:322
  74.6 1.7 %collective-permute-done.13.refs_1_ = bf16[1024,128]{1,0:T(8,128)(2,1)S(1)} collective-permute-done((bf16[1024,128]{1,0:T(8,128)(2,1)}, bf16[1024,128]{1,0:T(8,128)(2,1)S(1)}, u32[]{:S(2)}, u32[]{:S(2)}) %collective-permute-start.13) | collective-permute-done | bytes 262176 | tf_op jit(solution)/shard_map/ppermute | solution.py:322
  76.7 2.1 %collective-permute-start.6 = (bf16[1024,128]{1,0:T(8,128)(2,1)S(1)}, bf16[1024,128]{1,0:T(8,128)(2,1)S(1)}, u32[]{:S(2)}, u32[]{:S(2)}) collective-permute-start(bf16[1024,128]{1,0:T(8,128)(2,1)S(1)} %get-tuple-element.82), channel_id=1, source_target_pairs={{0,14},{1,15},{2,12},{3,13},{4,10},{5,11},{6,8},{7,9},{8,6},{9,7},... | collective-permute-start | bytes 786440 | tf_op jit(solution)/shard_map/ppermute | solution.py:322
  78.9 1.9 %collective-permute-done.7.refs_0_ = bf16[1024,128]{1,0:T(8,128)(2,1)S(1)} collective-permute-done((bf16[1024,128]{1,0:T(8,128)(2,1)S(1)}, bf16[1024,128]{1,0:T(8,128)(2,1)S(1)}, u32[]{:S(2)}, u32[]{:S(2)}) %collective-permute-start.7) | collective-permute-done | bytes 262176 | tf_op jit(solution)/shard_map/ppermute | solution.py:322
  80.8 2.3 %collective-permute-start.8 = (bf16[1024,128]{1,0:T(8,128)(2,1)S(1)}, bf16[1024,128]{1,0:T(8,128)(2,1)S(1)}, u32[]{:S(2)}, u32[]{:S(2)}) collective-permute-start(bf16[1024,128]{1,0:T(8,128)(2,1)S(1)} %get-tuple-element.87), channel_id=1, source_target_pairs={{0,15},{1,14},{2,13},{3,12},{4,11},{5,10},{6,9},{7,8},{8,7},{9,6},... | collective-permute-start | bytes 786440 | tf_op jit(solution)/shard_map/ppermute | solution.py:322
  83.1 6.1 %shard_map.69.refs_7_ = bf16[128,128,128]{2,1,0:T(8,128)(2,1)S(1)} custom-call(bf16[1024,128]{1,0:T(8,128)(2,1)S(1)} %collective-permute-done.9.refs_0_, bf16[1024,128]{1,0:T(8,128)(2,1)S(1)} %collective-permute-done.13.refs_1_, bf16[1024,128]{1,0:T(8,128)(2,1)S(1)} %collective-permute-done.11.refs_2_, bf16[1024,128]{1,0:T(8,128)(2,1)S(1)} %collective-permute-done.5.refs_3_, ...), custom_call_target="tpu_custom_call" | custom-call | flops 2415919104 | bytes 25165824 | tf_op jit(solution)/shard_map/pallas_call | solution.py:282
  89.3 15.4 %collective-permute-done.12.refs_2_ = bf16[1024,128]{1,0:T(8,128)(2,1)S(1)} collective-permute-done((bf16[1024,128]{1,0:T(8,128)(2,1)S(1)}, bf16[1024,128]{1,0:T(8,128)(2,1)S(1)}, u32[]{:S(2)}, u32[]{:S(2)}) %collective-permute-start.12) | collective-permute-done | bytes 262176 | tf_op jit(solution)/shard_map/ppermute | solution.py:322
  104.7 6.5 %collective-permute-done.14.refs_3_ = bf16[1024,128]{1,0:T(8,128)(2,1)S(1)} collective-permute-done((bf16[1024,128]{1,0:T(8,128)(2,1)S(1)}, bf16[1024,128]{1,0:T(8,128)(2,1)S(1)}, u32[]{:S(2)}, u32[]{:S(2)}) %collective-permute-start.14) | collective-permute-done | bytes 262176 | tf_op jit(solution)/shard_map/ppermute | solution.py:322
  111.1 6.2 %shard_map.70.refs_5_ = bf16[128,128,128]{2,1,0:T(8,128)(2,1)S(1)} custom-call(bf16[1024,128]{1,0:T(8,128)(2,1)S(1)} %collective-permute-done.7.refs_0_, bf16[1024,128]{1,0:T(8,128)(2,1)S(1)} %collective-permute-done.10.refs_1_, bf16[1024,128]{1,0:T(8,128)(2,1)S(1)} %collective-permute-done.12.refs_2_, ...), custom_call_target="tpu_custom_call" | custom-call | flops 2415919104 | bytes 25165824 | tf_op jit(solution)/shard_map/pallas_call | solution.py:282
  117.3 4.6 %collective-permute-done.8.refs_1_ = bf16[1024,128]{1,0:T(8,128)(2,1)S(1)} collective-permute-done((bf16[1024,128]{1,0:T(8,128)(2,1)S(1)}, bf16[1024,128]{1,0:T(8,128)(2,1)S(1)}, u32[]{:S(2)}, u32[]{:S(2)}) %collective-permute-start.8) | collective-permute-done | bytes 262176 | tf_op jit(solution)/shard_map/ppermute | solution.py:322
  121.9 6.2 %shard_map.71 = bf16[128,128,128]{2,1,0:T(8,128)(2,1)} custom-call(bf16[1024,128]{1,0:T(8,128)(2,1)S(1)} %collective-permute-done.6.refs_0_, bf16[1024,128]{1,0:T(8,128)(2,1)S(1)} %collective-permute-done.8.refs_1_, bf16[128,768]{1,0:T(8,128)(2,1)S(1)} %get-tuple-element.74.refs_6_.refs_4_.refs_2_, ...), custom_call_target="tpu_custom_call" | custom-call | flops 1207959552 | bytes 25165824 | tf_op jit(solution)/shard_map/pallas_call | solution.py:282
  (46 shorter events, 9.6 us)
Async XLA Ops:
  0.0 0.9 copy-start.1
  4.5 51.4 %all-to-all-start = ((bf16[16,144,128]{2,1,0:T(8,128)(2,1)}), bf16[16,144,128]{2,1,0:T(8,128)(2,1)S(1)}, u32[]{:S(2)}, u32[]{:S(2)}) async-start(bf16[16,144,128]{2,1,0:T(8,128)(2,1)} %shard_map.66), calls=%async_computation | async-start | bytes 1179648 | tf_op jit(solution)/shard_map/all_to_all | solution.py:327
  11.1 2.2 %copy-start = (bf16[16,1024,128]{2,1,0:T(8,128)(2,1)S(1)}, bf16[16,1024,128]{2,1,0:T(8,128)(2,1)}, u32[]{:S(2)}) copy-start(bf16[16,1024,128]{2,1,0:T(8,128)(2,1)} %source_ref.3) | copy-start | bytes 12582916
  13.9 41.9 %copy-start.5 = (s32[16]{0:T(128)S(1)}, s32[16]{0:T(128)}, u32[]{:S(2)}) copy-start(s32[16]{0:T(128)} %counts_ref.3) | copy-start | bytes 196
  13.9 41.9 %copy-start.6 = (f32[48]{0:T(128)S(1)}, f32[48]{0:T(128)}, u32[]{:S(2)}) copy-start(f32[48]{0:T(128)} %weights_ref.1) | copy-start | bytes 580
  14.8 7.5 %collective-permute-start = (bf16[1024,128]{1,0:T(8,128)(2,1)S(1)}, bf16[1024,128]{1,0:T(8,128)(2,1)S(1)}, u32[]{:S(2)}, u32[]{:S(2)}) collective-permute-start(bf16[1024,128]{1,0:T(8,128)(2,1)S(1)} %get-tuple-element.60), channel_id=1, source_target_pairs={{0,1},{1,0},{2,3},{3,2},{4,5},{5,4},{6,7},{7,6},{8,9},{9,8},{10,11... | collective-permute-start | bytes 786440 | tf_op jit(solution)/shard_map/ppermute | solution.py:322
  15.2 20.2 %collective-permute-start.1 = (bf16[1024,128]{1,0:T(8,128)(2,1)S(1)}, bf16[1024,128]{1,0:T(8,128)(2,1)S(1)}, u32[]{:S(2)}, u32[]{:S(2)}) collective-permute-start(bf16[1024,128]{1,0:T(8,128)(2,1)S(1)} %get-tuple-element.63), channel_id=1, source_target_pairs={{0,4},{1,5},{2,6},{3,7},{4,0},{5,1},{6,2},{7,3},{8,12},{9,13},{10,... | collective-permute-start | bytes 786440 | tf_op jit(solution)/shard_map/ppermute | solution.py:322
  15.2 25.9 %collective-permute-start.2 = (bf16[1024,128]{1,0:T(8,128)(2,1)S(1)}, bf16[1024,128]{1,0:T(8,128)(2,1)S(1)}, u32[]{:S(2)}, u32[]{:S(2)}) collective-permute-start(bf16[1024,128]{1,0:T(8,128)(2,1)S(1)} %get-tuple-element.66), channel_id=1, source_target_pairs={{0,5},{1,4},{2,7},{3,6},{4,1},{5,0},{6,3},{7,2},{8,13},{9,12},{10,... | collective-permute-start | bytes 786440 | tf_op jit(solution)/shard_map/ppermute | solution.py:322
  17.0 24.8 %collective-permute-start.3 = (bf16[1024,128]{1,0:T(8,128)(2,1)S(1)}, bf16[1024,128]{1,0:T(8,128)(2,1)S(1)}, u32[]{:S(2)}, u32[]{:S(2)}) collective-permute-start(bf16[1024,128]{1,0:T(8,128)(2,1)S(1)} %get-tuple-element.69), channel_id=1, source_target_pairs={{0,8},{1,9},{2,10},{3,11},{4,12},{5,13},{6,14},{7,15},{8,0},{9,1},... | collective-permute-start | bytes 786440 | tf_op jit(solution)/shard_map/ppermute | solution.py:322
  19.1 27.4 %collective-permute-start.4 = (bf16[1024,128]{1,0:T(8,128)(2,1)S(1)}, bf16[1024,128]{1,0:T(8,128)(2,1)S(1)}, u32[]{:S(2)}, u32[]{:S(2)}) collective-permute-start(bf16[1024,128]{1,0:T(8,128)(2,1)S(1)} %get-tuple-element.72), channel_id=1, source_target_pairs={{0,9},{1,8},{2,11},{3,10},{4,13},{5,12},{6,15},{7,14},{8,1},{9,0},... | collective-permute-start | bytes 786440 | tf_op jit(solution)/shard_map/ppermute | solution.py:322
  21.6 0.7 copy-start.17
  22.3 0.7 copy-start.7
  35.4 0.7 copy-start.9
  41.2 0.7 copy-start.11
  41.9 0.7 copy-start.13
  46.6 0.7 copy-start.15
  47.3 29.5 %collective-permute-start.5 = (bf16[1024,128]{1,0:T(8,128)(2,1)}, bf16[1024,128]{1,0:T(8,128)(2,1)S(1)}, u32[]{:S(2)}, u32[]{:S(2)}) collective-permute-start(bf16[1024,128]{1,0:T(8,128)(2,1)} %get-tuple-element.81), channel_id=1, source_target_pairs={{0,11},{1,10},{2,9},{3,8},{4,15},{5,14},{6,13},{7,12},{8,3},{9,2},... | collective-permute-start | bytes 786440 | tf_op jit(solution)/shard_map/ppermute | solution.py:322
  51.5 29.3 %collective-permute-start.7 = (bf16[1024,128]{1,0:T(8,128)(2,1)S(1)}, bf16[1024,128]{1,0:T(8,128)(2,1)S(1)}, u32[]{:S(2)}, u32[]{:S(2)}) collective-permute-start(bf16[1024,128]{1,0:T(8,128)(2,1)S(1)} %get-tuple-element.86), channel_id=1, source_target_pairs={{0,2},{1,3},{2,0},{3,1},{4,6},{5,7},{6,4},{7,5},{8,10},{9,11},{10,... | collective-permute-start | bytes 786440 | tf_op jit(solution)/shard_map/ppermute | solution.py:322
  51.8 21.0 %collective-permute-start.9 = (bf16[1024,128]{1,0:T(8,128)(2,1)}, bf16[1024,128]{1,0:T(8,128)(2,1)S(1)}, u32[]{:S(2)}, u32[]{:S(2)}) collective-permute-start(bf16[1024,128]{1,0:T(8,128)(2,1)} %get-tuple-element.90), channel_id=1, source_target_pairs={{0,6},{1,7},{2,4},{3,5},{4,2},{5,3},{6,0},{7,1},{8,14},{9,15},{10,... | collective-permute-start | bytes 786440 | tf_op jit(solution)/shard_map/ppermute | solution.py:322
  52.5 22.0 %collective-permute-start.11 = (bf16[1024,128]{1,0:T(8,128)(2,1)}, bf16[1024,128]{1,0:T(8,128)(2,1)S(1)}, u32[]{:S(2)}, u32[]{:S(2)}) collective-permute-start(bf16[1024,128]{1,0:T(8,128)(2,1)} %get-tuple-element.93), channel_id=1, source_target_pairs={{0,10},{1,11},{2,8},{3,9},{4,14},{5,15},{6,12},{7,13},{8,2},{9,3},... | collective-permute-start | bytes 786440 | tf_op jit(solution)/shard_map/ppermute | solution.py:322
  55.1 21.2 %collective-permute-start.13 = (bf16[1024,128]{1,0:T(8,128)(2,1)}, bf16[1024,128]{1,0:T(8,128)(2,1)S(1)}, u32[]{:S(2)}, u32[]{:S(2)}) collective-permute-start(bf16[1024,128]{1,0:T(8,128)(2,1)} %get-tuple-element.96), channel_id=1, source_target_pairs={{0,7},{1,6},{2,5},{3,4},{4,3},{5,2},{6,1},{7,0},{8,15},{9,14},{10,... | collective-permute-start | bytes 786440 | tf_op jit(solution)/shard_map/ppermute | solution.py:322
  57.5 1.0 copy-start.8
  58.5 0.9 copy-start.10
  59.4 0.9 copy-start.12
  60.4 0.9 copy-start.14
  61.3 0.9 copy-start.16
  62.3 0.9 copy-start.18
  72.9 16.4 %collective-permute-start.10 = (bf16[1024,128]{1,0:T(8,128)(2,1)S(1)}, bf16[1024,128]{1,0:T(8,128)(2,1)S(1)}, u32[]{:S(2)}, u32[]{:S(2)}) collective-permute-start(bf16[1024,128]{1,0:T(8,128)(2,1)S(1)} %get-tuple-element.91), channel_id=1, source_target_pairs={{0,3},{1,2},{2,1},{3,0},{4,7},{5,6},{6,5},{7,4},{8,11},{9,10},{10,... | collective-permute-start | bytes 786440 | tf_op jit(solution)/shard_map/ppermute | solution.py:322
  74.4 30.2 %collective-permute-start.12 = (bf16[1024,128]{1,0:T(8,128)(2,1)S(1)}, bf16[1024,128]{1,0:T(8,128)(2,1)S(1)}, u32[]{:S(2)}, u32[]{:S(2)}) collective-permute-start(bf16[1024,128]{1,0:T(8,128)(2,1)S(1)} %get-tuple-element.94), channel_id=1, source_target_pairs={{0,12},{1,13},{2,14},{3,15},{4,8},{5,9},{6,10},{7,11},{8,4},{9,5},... | collective-permute-start | bytes 786440 | tf_op jit(solution)/shard_map/ppermute | solution.py:322
  76.3 34.8 %collective-permute-start.14 = (bf16[1024,128]{1,0:T(8,128)(2,1)S(1)}, bf16[1024,128]{1,0:T(8,128)(2,1)S(1)}, u32[]{:S(2)}, u32[]{:S(2)}) collective-permute-start(bf16[1024,128]{1,0:T(8,128)(2,1)S(1)} %get-tuple-element.97), channel_id=1, source_target_pairs={{0,13},{1,12},{2,15},{3,14},{4,9},{5,8},{6,11},{7,10},{8,5},{9,4},... | collective-permute-start | bytes 786440 | tf_op jit(solution)/shard_map/ppermute | solution.py:322
  76.7 40.6 %collective-permute-start.6 = (bf16[1024,128]{1,0:T(8,128)(2,1)S(1)}, bf16[1024,128]{1,0:T(8,128)(2,1)S(1)}, u32[]{:S(2)}, u32[]{:S(2)}) collective-permute-start(bf16[1024,128]{1,0:T(8,128)(2,1)S(1)} %get-tuple-element.82), channel_id=1, source_target_pairs={{0,14},{1,15},{2,12},{3,13},{4,10},{5,11},{6,8},{7,9},{8,6},{9,7},... | collective-permute-start | bytes 786440 | tf_op jit(solution)/shard_map/ppermute | solution.py:322
  80.8 41.1 %collective-permute-start.8 = (bf16[1024,128]{1,0:T(8,128)(2,1)S(1)}, bf16[1024,128]{1,0:T(8,128)(2,1)S(1)}, u32[]{:S(2)}, u32[]{:S(2)}) collective-permute-start(bf16[1024,128]{1,0:T(8,128)(2,1)S(1)} %get-tuple-element.87), channel_id=1, source_target_pairs={{0,15},{1,14},{2,13},{3,12},{4,11},{5,10},{6,9},{7,8},{8,7},{9,6},... | collective-permute-start | bytes 786440 | tf_op jit(solution)/shard_map/ppermute | solution.py:322
  (3 other events, 2.0 us)

commit v3 on v2

--- a/solution.py
+++ b/solution.py
@@ -14,8 +14,8 @@
 ACC = jnp.bfloat16
 GROUPS = ((0, 2, 4), (3, 5), (1, 6), (7,))
 IN_FLIGHT = 5
-FAR_TURNS = (2, 4, 6, 8)
-HELD_BACK = 5
+FAR_TURNS = (2, 4, 5, 6, 10, 11)
+HELD_BACK = 0
 SMALL_VMEM = 16 * 1024 * 1024
 ROOM = 13 * 1024 * 1024
 
@@ -303,7 +303,8 @@
     per_unit = UNIT_ROWS * workers // extent
     half = workers // 2
     far = list(range(half, workers))
-    near = [1, *range(half // 2, half), *range(2, half // 2)]
+    upper, lower = list(range(half // 2, half)), list(range(2, half // 2))
+    near = [1, *upper[:-1], *lower[:1], upper[-1], *lower[1:]]
     order = []
     while far or near:
         take_far = far and (not near or len(order) in FAR_TURNS)

time: 129 us -> 133 us (1.031)
  the two profiles are of different devices: /device:TPU:11 before, /device:TPU:0 now
where the time goes in v3:
time: 133 us; the launch traced here: 132 us
  waiting for transfers between devices  57.6 us (43%)
  Pallas kernels  35.4 us (27%)
  starting transfers between devices  23.8 us (18%)
  local copies, waits for them, and re-layouts  15 us (11%)
    ppermute x15, waiting for transfers between devices, send(): lax.ppermute(piece, 'work', [(i, i ^ shift) for i in range(workers)])  57.6 us
    pallas_call x4, Pallas kernels, add_group(): pl.pallas_call(functools.partial(group_kernel, first, last, units, per_un...  28.6 us
    ppermute x15, starting transfers between devices, send(): lax.ppermute(piece, 'work', [(i, i ^ shift) for i in range(workers)])  16.4 us
    unnamed x38, local copies, waits for them, and re-layouts  15 us
    all_to_all x1, starting transfers between devices, per_device(): lax.all_to_all(matrices, 'work', split_axis=0, concat_axis=0, tiled=True)  7.38 us
    pallas_call x2, Pallas kernels, choose_pieces(): pl.pallas_call(functools.partial(pieces_kernel, shifts), in_specs=[pl.Blo...  2.93 us
  transfers between devices with their start and end apart: 16, of which 6 were waited for; matrix products, arithmetic and copies ran while one was open for 0% of the time, Pallas kernels for 20%

profile of v3, /device:TPU:0, one launch (start us, length us, event | category | flops | bytes accessed | tf_op | source)
XLA Modules:
  0.0 132.2 jit_solution(684193461258274449)
XLA Ops:
  0.0 0.9 copy-done.1
  2.3 2.2 %shard_map.66 = bf16[16,144,128]{2,1,0:T(8,128)(2,1)} custom-call(s32[16]{0:T(128)S(1)} %copy-done.4, s32[3,48]{1,0:T(4,128)S(1)} %bitcast.2, bf16[96,1024]{1,0:T(8,128)(2,1)S(1)} %copy-done.1), custom_call_target="tpu_custom_call" | custom-call | tf_op jit(solution)/shard_map/pallas_call | solution.py:90
  4.5 7.4 %all-to-all-start = ((bf16[16,144,128]{2,1,0:T(8,128)(2,1)}), bf16[16,144,128]{2,1,0:T(8,128)(2,1)S(1)}, u32[]{:S(2)}, u32[]{:S(2)}) async-start(bf16[16,144,128]{2,1,0:T(8,128)(2,1)} %shard_map.66), calls=%async_computation | async-start | bytes 1179648 | tf_op jit(solution)/shard_map/all_to_all | solution.py:328
  11.9 2.2 %copy-done = bf16[16,1024,128]{2,1,0:T(8,128)(2,1)S(1)} copy-done((bf16[16,1024,128]{2,1,0:T(8,128)(2,1)S(1)}, bf16[16,1024,128]{2,1,0:T(8,128)(2,1)}, u32[]{:S(2)}) %copy-start) | copy-done | bytes 4194328
  14.7 0.9 shard_map.65
  15.6 2.0 %collective-permute-start.12 = (bf16[1024,128]{1,0:T(8,128)(2,1)S(1)}, bf16[1024,128]{1,0:T(8,128)(2,1)S(1)}, u32[]{:S(2)}, u32[]{:S(2)}) collective-permute-start(bf16[1024,128]{1,0:T(8,128)(2,1)S(1)} %get-tuple-element.70), channel_id=1, source_target_pairs={{0,4},{1,5},{2,6},{3,7},{4,0},{5,1},{6,2},{7,3},{8,12},{9,13},{10,... | collective-permute-start | bytes 786440 | tf_op jit(solution)/shard_map/ppermute | solution.py:323
  17.6 2.4 %collective-permute-start.6 = (bf16[1024,128]{1,0:T(8,128)(2,1)S(1)}, bf16[1024,128]{1,0:T(8,128)(2,1)S(1)}, u32[]{:S(2)}, u32[]{:S(2)}) collective-permute-start(bf16[1024,128]{1,0:T(8,128)(2,1)S(1)} %get-tuple-element.60), channel_id=1, source_target_pairs={{0,8},{1,9},{2,10},{3,11},{4,12},{5,13},{6,14},{7,15},{8,0},{9,1},... | collective-permute-start | bytes 786440 | tf_op jit(solution)/shard_map/ppermute | solution.py:323
  20.5 2.1 %shard_map.64 = (bf16[1024,128]{1,0:T(8,128)(2,1)S(1)}, bf16[1024,128]{1,0:T(8,128)(2,1)S(1)}, bf16[1024,128]{1,0:T(8,128)(2,1)S(1)}, bf16[1024,128]{1,0:T(8,128...) custom-call(s32[16]{0:T(128)S(1)} %copy-done.3, ...), custom_call_target="tpu_custom_call" | custom-call | tf_op jit(solution)/shard_map/pallas_call | solution.py:43
  23.2 10.8 %collective-permute-done.12.refs_2_ = bf16[1024,128]{1,0:T(8,128)(2,1)S(1)} collective-permute-done((bf16[1024,128]{1,0:T(8,128)(2,1)S(1)}, bf16[1024,128]{1,0:T(8,128)(2,1)S(1)}, u32[]{:S(2)}, u32[]{:S(2)}) %collective-permute-start.12) | collective-permute-done | bytes 262176 | tf_op jit(solution)/shard_map/ppermute | solution.py:323
  35.5 2.6 %collective-permute-start.10 = (bf16[1024,128]{1,0:T(8,128)(2,1)S(1)}, bf16[1024,128]{1,0:T(8,128)(2,1)S(1)}, u32[]{:S(2)}, u32[]{:S(2)}) collective-permute-start(bf16[1024,128]{1,0:T(8,128)(2,1)S(1)} %get-tuple-element.66), channel_id=1, source_target_pairs={{0,10},{1,11},{2,8},{3,9},{4,14},{5,15},{6,12},{7,13},{8,2},{9,3},... | collective-permute-start | bytes 786440 | tf_op jit(solution)/shard_map/ppermute | solution.py:323
  38.1 7.9 %collective-permute-done.6.refs_4_ = bf16[1024,128]{1,0:T(8,128)(2,1)S(1)} collective-permute-done((bf16[1024,128]{1,0:T(8,128)(2,1)S(1)}, bf16[1024,128]{1,0:T(8,128)(2,1)S(1)}, u32[]{:S(2)}, u32[]{:S(2)}) %collective-permute-start.6) | collective-permute-done | bytes 262176 | tf_op jit(solution)/shard_map/ppermute | solution.py:323
  46.6 15.2 %collective-permute-done.3.refs_5_ = bf16[1024,128]{1,0:T(8,128)(2,1)S(1)} collective-permute-done((bf16[1024,128]{1,0:T(8,128)(2,1)S(1)}, bf16[1024,128]{1,0:T(8,128)(2,1)S(1)}, u32[]{:S(2)}, u32[]{:S(2)}) %collective-permute-start.3) | collective-permute-done | bytes 262176 | tf_op jit(solution)/shard_map/ppermute | solution.py:323
  61.8 0.7 copy-done.13
  62.6 0.7 copy-done.15
  63.3 1.5 %collective-permute-start.1 = (bf16[1024,128]{1,0:T(8,128)(2,1)S(1)}, bf16[1024,128]{1,0:T(8,128)(2,1)S(1)}, u32[]{:S(2)}, u32[]{:S(2)}) collective-permute-start(bf16[1024,128]{1,0:T(8,128)(2,1)S(1)} %get-tuple-element.47), channel_id=1, source_target_pairs={{0,2},{1,3},{2,0},{3,1},{4,6},{5,7},{6,4},{7,5},{8,10},{9,11},{10,... | collective-permute-start | bytes 786440 | tf_op jit(solution)/shard_map/ppermute | solution.py:323
  64.8 3.8 %collective-permute-done.13.refs_3_ = bf16[1024,128]{1,0:T(8,128)(2,1)S(1)} collective-permute-done((bf16[1024,128]{1,0:T(8,128)(2,1)S(1)}, bf16[1024,128]{1,0:T(8,128)(2,1)S(1)}, u32[]{:S(2)}, u32[]{:S(2)}) %collective-permute-start.13) | collective-permute-done | bytes 262176 | tf_op jit(solution)/shard_map/ppermute | solution.py:323
  68.6 1.6 %collective-permute-start.14 = (bf16[1024,128]{1,0:T(8,128)(2,1)}, bf16[1024,128]{1,0:T(8,128)(2,1)S(1)}, u32[]{:S(2)}, u32[]{:S(2)}) collective-permute-start(bf16[1024,128]{1,0:T(8,128)(2,1)} %get-tuple-element.72), channel_id=1, source_target_pairs={{0,13},{1,12},{2,15},{3,14},{4,9},{5,8},{6,11},{7,10},{8,5},{9,4},... | collective-permute-start | bytes 786440 | tf_op jit(solution)/shard_map/ppermute | solution.py:323
  70.3 13.2 %collective-permute-done.10.refs_2_ = bf16[1024,128]{1,0:T(8,128)(2,1)S(1)} collective-permute-done((bf16[1024,128]{1,0:T(8,128)(2,1)S(1)}, bf16[1024,128]{1,0:T(8,128)(2,1)S(1)}, u32[]{:S(2)}, u32[]{:S(2)}) %collective-permute-start.10) | collective-permute-done | bytes 262176 | tf_op jit(solution)/shard_map/ppermute | solution.py:323
  83.5 1.3 collective-permute-start.11
  84.8 6.6 %collective-permute-done.4.refs_1_ = bf16[1024,128]{1,0:T(8,128)(2,1)S(1)} collective-permute-done((bf16[1024,128]{1,0:T(8,128)(2,1)S(1)}, bf16[1024,128]{1,0:T(8,128)(2,1)S(1)}, u32[]{:S(2)}, u32[]{:S(2)}) %collective-permute-start.4) | collective-permute-done | bytes 262176 | tf_op jit(solution)/shard_map/ppermute | solution.py:323
  91.4 4.5 %collective-permute-start.2 = (bf16[1024,128]{1,0:T(8,128)(2,1)S(1)}, bf16[1024,128]{1,0:T(8,128)(2,1)S(1)}, u32[]{:S(2)}, u32[]{:S(2)}) collective-permute-start(bf16[1024,128]{1,0:T(8,128)(2,1)S(1)} %get-tuple-element.48), channel_id=1, source_target_pairs={{0,14},{1,15},{2,12},{3,13},{4,10},{5,11},{6,8},{7,9},{8,6},{9,7},... | collective-permute-start | bytes 786440 | tf_op jit(solution)/shard_map/ppermute | solution.py:323
  95.9 1.7 %shard_map.67 = (bf16[128,768]{1,0:T(8,128)(2,1)S(1)}, bf16[768,128]{1,0:T(8,128)(2,1)S(1)}, bf16[8,96,128]{2,1,0:T(8,128)(2,1)S(1)}) custom-call(s32[16]{0:T(128)S(1)} %copy-done.5, f32[48]{0:T(128)S(1)} %copy-done.6, bf16[16,144,128]{2,1,0:T(8,128)(2,1)S(1)} %all-to-all-done.matrix_ref), custom_call_target="tpu_custom_call" | custom-call | tf_op jit(solution)/shard_map/pallas_call | solution.py:146
  97.6 0.9 copy-done.8
  98.5 0.9 copy-done.10
  99.5 0.9 copy-done.12
  100.4 0.9 copy-done.14
  101.4 0.9 copy-done.16
  102.3 0.9 copy-done.18
  103.3 9.6 %shard_map.68.refs_7_ = bf16[128,128,128]{2,1,0:T(8,128)(2,1)S(1)} custom-call(bf16[1024,128]{1,0:T(8,128)(2,1)S(1)} %copy-done.18, bf16[1024,128]{1,0:T(8,128)(2,1)S(1)} %copy-done.10, bf16[1024,128]{1,0:T(8,128)(2,1)S(1)} %copy-done.8, bf16[1024,128]{1,0:T(8,128)(2,1)S(1)} %copy-done.16, bf16[1024,128]{1,0:T(8,128)(2,1)S(1)} %copy-done.12, ...), custom_call_target="tpu_custom_call" | custom-call | flops 3623878656 | bytes 25165824 | tf_op jit(solution)/shard_map/pallas_call | solution.py:282
  112.9 6.3 %shard_map.69.refs_7_ = bf16[128,128,128]{2,1,0:T(8,128)(2,1)S(1)} custom-call(bf16[1024,128]{1,0:T(8,128)(2,1)S(1)} %collective-permute-done.7.refs_0_, bf16[1024,128]{1,0:T(8,128)(2,1)S(1)} %collective-permute-done.4.refs_1_, bf16[1024,128]{1,0:T(8,128)(2,1)S(1)} %collective-permute-done.10.refs_2_, bf16[1024,128]{1,0:T(8,128)(2,1)S(1)} %collective-permute-done.13.refs_3_, ...), custom_call_target="tpu_custom_call" | custom-call | flops 2415919104 | bytes 25165824 | tf_op jit(solution)/shard_map/pallas_call | solution.py:282
  119.3 6.2 %shard_map.70.refs_5_ = bf16[128,128,128]{2,1,0:T(8,128)(2,1)S(1)} custom-call(bf16[1024,128]{1,0:T(8,128)(2,1)S(1)} %collective-permute-done.1.refs_0_, bf16[1024,128]{1,0:T(8,128)(2,1)S(1)} %collective-permute-done.8.refs_1_, bf16[1024,128]{1,0:T(8,128)(2,1)S(1)} %collective-permute-done.11.refs_2_, bf16[1024,128]{1,0:T(8,128)(2,1)S(1)} %collective-permute-done.14.refs_3_, ...), custom_call_target="tpu_custom_call" | custom-call | flops 2415919104 | bytes 25165824 | tf_op jit(solution)/shard_map/pallas_call | solution.py:282
  125.5 6.5 %shard_map.71 = bf16[128,128,128]{2,1,0:T(8,128)(2,1)} custom-call(bf16[1024,128]{1,0:T(8,128)(2,1)S(1)} %collective-permute-done.2.refs_0_, bf16[1024,128]{1,0:T(8,128)(2,1)S(1)} %collective-permute-done.5.refs_1_, bf16[128,768]{1,0:T(8,128)(2,1)S(1)} %get-tuple-element.54.refs_6_.refs_4_.refs_2_, ...), custom_call_target="tpu_custom_call" | custom-call | flops 1207959552 | bytes 25165824 | tf_op jit(solution)/shard_map/pallas_call | solution.py:282
  (46 shorter events, 5.4 us)
Async XLA Ops:
  0.0 0.9 copy-start.1
  4.5 91.4 %all-to-all-start = ((bf16[16,144,128]{2,1,0:T(8,128)(2,1)}), bf16[16,144,128]{2,1,0:T(8,128)(2,1)S(1)}, u32[]{:S(2)}, u32[]{:S(2)}) async-start(bf16[16,144,128]{2,1,0:T(8,128)(2,1)} %shard_map.66), calls=%async_computation | async-start | bytes 1179648 | tf_op jit(solution)/shard_map/all_to_all | solution.py:328
  11.9 2.2 %copy-start = (bf16[16,1024,128]{2,1,0:T(8,128)(2,1)S(1)}, bf16[16,1024,128]{2,1,0:T(8,128)(2,1)}, u32[]{:S(2)}) copy-start(bf16[16,1024,128]{2,1,0:T(8,128)(2,1)} %source_ref.3) | copy-start | bytes 12582916
  14.7 81.2 %copy-start.5 = (s32[16]{0:T(128)S(1)}, s32[16]{0:T(128)}, u32[]{:S(2)}) copy-start(s32[16]{0:T(128)} %counts_ref.3) | copy-start | bytes 196
  14.7 81.2 %copy-start.6 = (f32[48]{0:T(128)S(1)}, f32[48]{0:T(128)}, u32[]{:S(2)}) copy-start(f32[48]{0:T(128)} %weights_ref.1) | copy-start | bytes 580
  15.6 18.5 %collective-permute-start.12 = (bf16[1024,128]{1,0:T(8,128)(2,1)S(1)}, bf16[1024,128]{1,0:T(8,128)(2,1)S(1)}, u32[]{:S(2)}, u32[]{:S(2)}) collective-permute-start(bf16[1024,128]{1,0:T(8,128)(2,1)S(1)} %get-tuple-element.70), channel_id=1, source_target_pairs={{0,4},{1,5},{2,6},{3,7},{4,0},{5,1},{6,2},{7,3},{8,12},{9,13},{10,... | collective-permute-start | bytes 786440 | tf_op jit(solution)/shard_map/ppermute | solution.py:323
  17.6 17.2 %collective-permute-start.9 = (bf16[1024,128]{1,0:T(8,128)(2,1)S(1)}, bf16[1024,128]{1,0:T(8,128)(2,1)S(1)}, u32[]{:S(2)}, u32[]{:S(2)}) collective-permute-start(bf16[1024,128]{1,0:T(8,128)(2,1)S(1)} %get-tuple-element.65), channel_id=1, source_target_pairs={{0,1},{1,0},{2,3},{3,2},{4,5},{5,4},{6,7},{7,6},{8,9},{9,8},{10,11... | collective-permute-start | bytes 786440 | tf_op jit(solution)/shard_map/ppermute | solution.py:323
  17.6 28.4 %collective-permute-start.6 = (bf16[1024,128]{1,0:T(8,128)(2,1)S(1)}, bf16[1024,128]{1,0:T(8,128)(2,1)S(1)}, u32[]{:S(2)}, u32[]{:S(2)}) collective-permute-start(bf16[1024,128]{1,0:T(8,128)(2,1)S(1)} %get-tuple-element.60), channel_id=1, source_target_pairs={{0,8},{1,9},{2,10},{3,11},{4,12},{5,13},{6,14},{7,15},{8,0},{9,1},... | collective-permute-start | bytes 786440 | tf_op jit(solution)/shard_map/ppermute | solution.py:323
  19.9 41.9 %collective-permute-start.3 = (bf16[1024,128]{1,0:T(8,128)(2,1)S(1)}, bf16[1024,128]{1,0:T(8,128)(2,1)S(1)}, u32[]{:S(2)}, u32[]{:S(2)}) collective-permute-start(bf16[1024,128]{1,0:T(8,128)(2,1)S(1)} %get-tuple-element.51), channel_id=1, source_target_pairs={{0,9},{1,8},{2,11},{3,10},{4,13},{5,12},{6,15},{7,14},{8,1},{9,0},... | collective-permute-start | bytes 786440 | tf_op jit(solution)/shard_map/ppermute | solution.py:323
  20.3 42.3 %collective-permute-start = (bf16[1024,128]{1,0:T(8,128)(2,1)S(1)}, bf16[1024,128]{1,0:T(8,128)(2,1)S(1)}, u32[]{:S(2)}, u32[]{:S(2)}) collective-permute-start(bf16[1024,128]{1,0:T(8,128)(2,1)S(1)} %get-tuple-element.46), channel_id=1, source_target_pairs={{0,5},{1,4},{2,7},{3,6},{4,1},{5,0},{6,3},{7,2},{8,13},{9,12},{10,... | collective-permute-start | bytes 786440 | tf_op jit(solution)/shard_map/ppermute | solution.py:323
  22.6 0.7 copy-start.17
  34.1 0.7 copy-start.7
  34.8 33.8 %collective-permute-start.13 = (bf16[1024,128]{1,0:T(8,128)(2,1)S(1)}, bf16[1024,128]{1,0:T(8,128)(2,1)S(1)}, u32[]{:S(2)}, u32[]{:S(2)}) collective-permute-start(bf16[1024,128]{1,0:T(8,128)(2,1)S(1)} %get-tuple-element.71), channel_id=1, source_target_pairs={{0,11},{1,10},{2,9},{3,8},{4,15},{5,14},{6,13},{7,12},{8,3},{9,2},... | collective-permute-start | bytes 786440 | tf_op jit(solution)/shard_map/ppermute | solution.py:323
  34.8 0.7 copy-start.9
  35.5 48.0 %collective-permute-start.10 = (bf16[1024,128]{1,0:T(8,128)(2,1)S(1)}, bf16[1024,128]{1,0:T(8,128)(2,1)S(1)}, u32[]{:S(2)}, u32[]{:S(2)}) collective-permute-start(bf16[1024,128]{1,0:T(8,128)(2,1)S(1)} %get-tuple-element.66), channel_id=1, source_target_pairs={{0,10},{1,11},{2,8},{3,9},{4,14},{5,15},{6,12},{7,13},{8,2},{9,3},... | collective-permute-start | bytes 786440 | tf_op jit(solution)/shard_map/ppermute | solution.py:323
  45.9 0.7 copy-start.11
  46.6 38.1 %collective-permute-start.7 = (bf16[1024,128]{1,0:T(8,128)(2,1)S(1)}, bf16[1024,128]{1,0:T(8,128)(2,1)S(1)}, u32[]{:S(2)}, u32[]{:S(2)}) collective-permute-start(bf16[1024,128]{1,0:T(8,128)(2,1)S(1)} %get-tuple-element.61), channel_id=1, source_target_pairs={{0,6},{1,7},{2,4},{3,5},{4,2},{5,3},{6,0},{7,1},{8,14},{9,15},{10,... | collective-permute-start | bytes 786440 | tf_op jit(solution)/shard_map/ppermute | solution.py:323
  61.8 0.7 copy-start.13
  62.6 28.8 %collective-permute-start.4 = (bf16[1024,128]{1,0:T(8,128)(2,1)S(1)}, bf16[1024,128]{1,0:T(8,128)(2,1)S(1)}, u32[]{:S(2)}, u32[]{:S(2)}) collective-permute-start(bf16[1024,128]{1,0:T(8,128)(2,1)S(1)} %get-tuple-element.52), channel_id=1, source_target_pairs={{0,7},{1,6},{2,5},{3,4},{4,3},{5,2},{6,1},{7,0},{8,15},{9,14},{10,... | collective-permute-start | bytes 786440 | tf_op jit(solution)/shard_map/ppermute | solution.py:323
  62.6 0.7 copy-start.15
  63.3 28.1 %collective-permute-start.1 = (bf16[1024,128]{1,0:T(8,128)(2,1)S(1)}, bf16[1024,128]{1,0:T(8,128)(2,1)S(1)}, u32[]{:S(2)}, u32[]{:S(2)}) collective-permute-start(bf16[1024,128]{1,0:T(8,128)(2,1)S(1)} %get-tuple-element.47), channel_id=1, source_target_pairs={{0,2},{1,3},{2,0},{3,1},{4,6},{5,7},{6,4},{7,5},{8,10},{9,11},{10,... | collective-permute-start | bytes 786440 | tf_op jit(solution)/shard_map/ppermute | solution.py:323
  68.6 50.7 %collective-permute-start.14 = (bf16[1024,128]{1,0:T(8,128)(2,1)}, bf16[1024,128]{1,0:T(8,128)(2,1)S(1)}, u32[]{:S(2)}, u32[]{:S(2)}) collective-permute-start(bf16[1024,128]{1,0:T(8,128)(2,1)} %get-tuple-element.72), channel_id=1, source_target_pairs={{0,13},{1,12},{2,15},{3,14},{4,9},{5,8},{6,11},{7,10},{8,5},{9,4},... | collective-permute-start | bytes 786440 | tf_op jit(solution)/shard_map/ppermute | solution.py:323
  83.5 35.8 %collective-permute-start.11 = (bf16[1024,128]{1,0:T(8,128)(2,1)}, bf16[1024,128]{1,0:T(8,128)(2,1)S(1)}, u32[]{:S(2)}, u32[]{:S(2)}) collective-permute-start(bf16[1024,128]{1,0:T(8,128)(2,1)} %get-tuple-element.67), channel_id=1, source_target_pairs={{0,12},{1,13},{2,14},{3,15},{4,8},{5,9},{6,10},{7,11},{8,4},{9,5},... | collective-permute-start | bytes 786440 | tf_op jit(solution)/shard_map/ppermute | solution.py:323
  84.8 34.5 %collective-permute-start.8 = (bf16[1024,128]{1,0:T(8,128)(2,1)}, bf16[1024,128]{1,0:T(8,128)(2,1)S(1)}, u32[]{:S(2)}, u32[]{:S(2)}) collective-permute-start(bf16[1024,128]{1,0:T(8,128)(2,1)} %get-tuple-element.62), channel_id=1, source_target_pairs={{0,3},{1,2},{2,1},{3,0},{4,7},{5,6},{6,5},{7,4},{8,11},{9,10},{10,... | collective-permute-start | bytes 786440 | tf_op jit(solution)/shard_map/ppermute | solution.py:323
  91.4 34.1 %collective-permute-start.5 = (bf16[1024,128]{1,0:T(8,128)(2,1)}, bf16[1024,128]{1,0:T(8,128)(2,1)S(1)}, u32[]{:S(2)}, u32[]{:S(2)}) collective-permute-start(bf16[1024,128]{1,0:T(8,128)(2,1)} %get-tuple-element.53), channel_id=1, source_target_pairs={{0,15},{1,14},{2,13},{3,12},{4,11},{5,10},{6,9},{7,8},{8,7},{9,6},... | collective-permute-start | bytes 786440 | tf_op jit(solution)/shard_map/ppermute | solution.py:323
  91.4 34.1 %collective-permute-start.2 = (bf16[1024,128]{1,0:T(8,128)(2,1)S(1)}, bf16[1024,128]{1,0:T(8,128)(2,1)S(1)}, u32[]{:S(2)}, u32[]{:S(2)}) collective-permute-start(bf16[1024,128]{1,0:T(8,128)(2,1)S(1)} %get-tuple-element.48), channel_id=1, source_target_pairs={{0,14},{1,15},{2,12},{3,13},{4,10},{5,11},{6,8},{7,9},{8,6},{9,7},... | collective-permute-start | bytes 786440 | tf_op jit(solution)/shard_map/ppermute | solution.py:323
  97.6 1.0 copy-start.8
  98.5 0.9 copy-start.10
  99.5 0.9 copy-start.12
  100.4 0.9 copy-start.14
  101.4 0.9 copy-start.16
  102.3 0.9 copy-start.18
  (3 other events, 2.0 us)
